TPU v7x, 32 devices: a whole 2x2x4 slice. The times are simulated.
32 devices in a mesh: slab: 4 (over y, core), col: 8 (over z, x).
Axes of the slice: x: 2, y: 2, z: 4, core: 2. Of those that a mesh axis runs over, the one named last changes fastest.
Arguments:
- load: float32 [3, 64, 128, 128], P(None, 'slab', 'col'), may hold values from -6 to 6
- density: int32 [64, 128, 128], P('slab', 'col'), may hold values from 0 to 7
- moduli: float32 [8], replicated, may hold values from 0.1 to 10
- fixed: int32 [64, 128, 128], P('slab', 'col'), may hold values 0 or 1
Outputs:
- solution_field: float32 [3, 64, 128, 128], P(None, 'slab', 'col')
- residual: float32 [3, 64, 128, 128], P(None, 'slab', 'col')
All inputs are finite; a program needn't handle non-finite values. No bound on the sum of `fixed` on one device may be relied on, other than what follows from the above.
Results may differ from a plain program's by a relative error of at most 0.0001.
Values sent between devices are 32-bit elements; how exact they have to be, the bound alone decides.
A program may use at most 128 MiB of HBM per device.

v0:
```python
import jax
import jax.numpy as jnp
from jax import lax
from jax.sharding import PartitionSpec as P

LEVELS = 3
PRE = 2
POST = 2
COARSE_SWEEPS = 8
CLASSES = 8


OMEGA = 0.6
COUPLE = 0.05


def padded_2(block, sides, width):
    for axis, dim in sides:
        count = lax.axis_size(axis)
        forward = [(i, i + 1) for i in range(count - 1)]
        backward = [(target, source) for source, target in forward]
        low = lax.ppermute(
            lax.slice_in_dim(block, block.shape[dim] - width, None, axis=dim), axis, forward
        )
        high = lax.ppermute(lax.slice_in_dim(block, 0, width, axis=dim), axis, backward)
        block = jnp.concatenate([low, block, high], axis=dim)
    return block


def shrink(arr):
    lead = arr.shape[:-3]
    za, yb, xc = arr.shape[-3:]
    blocks = arr.reshape(tuple(lead) + (za // 2, 2, yb // 2, 2, xc // 2, 2))
    return blocks.mean(axis=(-5, -3, -1))


def grow(arr):
    return jnp.repeat(jnp.repeat(jnp.repeat(arr, 2, axis=-3), 2, axis=-2), 2, axis=-1)


def beside_all(padded):
    return [
        padded[..., 2:, 1:-1, 1:-1],
        padded[..., :-2, 1:-1, 1:-1],
        padded[..., 1:-1, 2:, 1:-1],
        padded[..., 1:-1, :-2, 1:-1],
        padded[..., 1:-1, 1:-1, 2:],
        padded[..., 1:-1, 1:-1, :-2],
    ]


def diagonal_of(stiff_pad, scale):
    centre = stiff_pad[1:-1, 1:-1, 1:-1]
    total = jnp.zeros_like(centre)
    for near in beside_all(stiff_pad):
        total = total + 0.5 * (centre + near)
    return scale * total + 2.0 * COUPLE * centre


def apply_op(field_pad, stiff_pad, scale):
    centre = stiff_pad[1:-1, 1:-1, 1:-1]
    field = field_pad[:, 1:-1, 1:-1, 1:-1]
    total = jnp.zeros_like(field)
    for near_k, near_u in zip(beside_all(stiff_pad), beside_all(field_pad)):
        total = total + 0.5 * (centre + near_k) * (field - near_u)
    return scale * total + COUPLE * centre * (field + jnp.sum(field, axis=0, keepdims=True))


def pad_xdim(padded):
    return jnp.pad(padded, ((0, 0), (0, 0), (0, 0), (1, 1)))


def field_extended(field):
    return pad_xdim(padded_2(field, (("slab", 1), ("col", 2)), 1))


def coarse_extended(field):
    return pad_xdim(padded_2(field, (("slab", 1), ("col", 2)), 1))


def sweeps(field, rhs, stiff_pad, diag, scale, weight, count, extend):
    if field is None:
        field = OMEGA * weight * rhs / diag
        count = count - 1
    for turn in range(count):
        field = field + OMEGA * weight * (rhs - apply_op(extend(field), stiff_pad, scale)) / diag
    return field


def on_device(load, density, moduli, fixed):
    stiff = jnp.zeros(density.shape, jnp.float32)
    for klass in range(CLASSES):
        stiff = stiff + jnp.where(density == klass, moduli[klass], jnp.float32(0.0))
    mask = 1.0 - fixed.astype(jnp.float32)
    pads = []
    current = stiff
    for level in range(LEVELS + 1):
        rimmed = padded_2(current, (("slab", 0), ("col", 1)), 1)
        pads.append(jnp.pad(rimmed, ((0, 0), (0, 0), (1, 1))))
        if level < LEVELS:
            current = shrink(current)
    diags = [diagonal_of(pads[level], 0.25**level) for level in range(LEVELS + 1)]
    saved = []
    rhs = load
    for level in range(LEVELS):
        weight = mask if level == 0 else 1.0
        scale = 0.25**level
        field = sweeps(None, rhs, pads[level], diags[level], scale, weight, PRE, field_extended)
        resid = weight * (rhs - apply_op(field_extended(field), pads[level], scale))
        saved.append((field, rhs))
        rhs = shrink(resid)
    coarse_scale = 0.25**LEVELS
    field = sweeps(
        None, rhs, pads[LEVELS], diags[LEVELS], coarse_scale, 1.0, COARSE_SWEEPS, coarse_extended
    )
    for level in range(LEVELS - 1, -1, -1):
        weight = mask if level == 0 else 1.0
        fine, rhs = saved[level]
        field = fine + weight * grow(field)
        field = sweeps(
            field, rhs, pads[level], diags[level], 0.25**level, weight, POST, field_extended
        )
    residual = mask * (load - apply_op(field_extended(field), pads[0], 1.0))
    return (field, residual)


def solution(mesh):
    placed = (P(None, "slab", "col", None), P("slab", "col", None), P(), P("slab", "col", None))
    return jax.shard_map(
        on_device,
        mesh=mesh,
        in_specs=placed,
        out_specs=(P(None, "slab", "col", None), P(None, "slab", "col", None)),
        check_vma=False,
    )
```

profile of v0, /device:TPU:28, one launch (start us, length us, event | category | flops | bytes accessed | tf_op | source)
XLA Modules:
  0.0 439.1 jit_solution(17269869428800374154)
XLA Ops:
  2.3 6.1 %convert_subtract_fusion = (f32[16,16,128]{2,1,0:T(8,128)S(1)}, f32[16,16,128]{2,1,0:T(8,128)S(1)}, f32[16,16,128]{2,1,0:T(8,128)S(1)}, f32[16,16,128]{2,1,0:T(8,128)S(1)}) fusion(s32[16,16,128]{2,1,0:T(8,128)} %param.7, f32[]{:T(128)} %bitcast.7, s32[16,16,128]{2,1,0:T(8,128)} %param.5, f32[]{:T(128)} %bitcast.6, f32[]{:T(128)} %bitcast.5, f32[]{:T(128)} %bitcast.4, ...), kind=kLoop, calls=%fused_computation.219 | loop fusion | flops 884736 | bytes 786464 | tf_op jit(solution)/shard_map/sub | solution.py:94
  12.7 9.8 %reshape.112 = f32[8,2,8,2,64,2]{5,4,3,2,1,0:T(8,128)} reshape(f32[16,16,128]{2,1,0:T(8,128)S(1)} %get-tuple-element.192) | data formatting | bytes 262144 | tf_op jit(solution)/shard_map/reshape | solution.py:33
  22.5 4.0 reduce_sum.237
  26.6 3.2 collective-permute-start.12
  32.9 3.6 collective-permute-start.24
  36.9 3.3 collective-permute-start.2
  40.2 2.6 collective-permute-start.3
  51.5 3.5 collective-permute-start.14
  55.1 3.2 collective-permute-start.6
  58.3 2.7 collective-permute-start.7
  70.7 2.6 collective-permute-done.9
  73.3 3.5 collective-permute-start.10
  79.3 4.1 collective-permute-done.11
  84.7 26.5 %reshape.111 = f32[3,8,2,8,2,64,2]{6,5,4,3,2,1,0:T(8,128)} reshape(f32[3,16,16,128]{3,2,1,0:T(8,128)S(1)} %fusion.64) | data formatting | bytes 786432 | tf_op jit(solution)/shard_map/reshape | solution.py:33
  111.2 9.4 %reduce_sum.236 = f32[3,8,8,64]{3,2,1,0:T(8,128)S(1)} reduce(f32[3,8,2,8,2,64,2]{6,5,4,3,2,1,0:T(8,128)} %reshape.111, f32[]{:T(128)} %constant.24.clone.1), dimensions={2,4,6}, to_apply=%region_2.3 | reduce | flops 86016 | bytes 442372 | tf_op jit(solution)/shard_map/reduce_sum | solution.py:34
  125.7 3.1 collective-permute-start.36
  132.8 3.9 collective-permute-start.19
  136.7 2.8 collective-permute-start.26
  139.6 3.0 collective-permute-start.27
  143.0 2.5 collective-permute-start.20
  147.6 3.0 collective-permute-done.21
  150.6 4.0 collective-permute-start.22
  157.4 3.7 collective-permute-done.23
  162.2 4.1 reshape.113
  176.8 3.9 collective-permute-start.31
  180.8 2.8 collective-permute-start.38
  183.6 3.0 collective-permute-start.39
  194.6 3.7 collective-permute-start.34
  201.4 3.5 collective-permute-done.35
  210.6 2.5 collective-permute-done.41
  215.1 3.9 collective-permute-start.43
  226.1 2.5 collective-permute-done.45
  228.6 2.9 collective-permute-start.46
  231.5 2.9 collective-permute-start.47
  234.5 3.5 collective-permute-done.47
  242.5 2.5 collective-permute-done.49
  247.0 3.9 collective-permute-start.51
  258.0 2.5 collective-permute-done.53
  260.5 2.9 collective-permute-start.54
  263.4 2.9 collective-permute-start.55
  266.4 3.5 collective-permute-done.55
  278.9 3.9 collective-permute-start.59
  294.3 3.9 collective-permute-start.63
  309.8 3.9 collective-permute-start.67
  321.2 2.5 collective-permute-done.69
  325.7 3.9 collective-permute-start.71
  329.6 2.5 collective-permute-done.71
  336.8 2.5 collective-permute-done.73
  341.3 3.9 collective-permute-start.75
  345.2 2.5 collective-permute-done.75
  353.3 2.6 collective-permute-done.77
  357.8 3.9 collective-permute-start.79
  361.8 2.6 collective-permute-done.79
  369.2 2.6 collective-permute-done.81
  373.7 3.9 collective-permute-start.83
  377.7 2.6 collective-permute-done.83
  391.8 2.7 collective-permute-done.85
  396.5 4.1 collective-permute-start.87
  408.8 2.7 collective-permute-done.89
  413.5 3.9 collective-permute-start.91
  417.4 2.7 collective-permute-done.91
  425.9 2.7 collective-permute-done.93
  430.5 3.9 collective-permute-start.95
  434.5 2.7 collective-permute-done.95
  (378 shorter events, 190.5 us)
Async XLA Ops:
  8.4 28.4 %collective-permute-start = (f32[1,16,128]{2,1,0:T(8,128)S(1)}, f32[1,16,128]{2,1,0:T(8,128)S(1)}, u32[]{:S(2)}, u32[]{:S(2)}) collective-permute-start(f32[1,16,128]{2,1,0:T(8,128)S(1)} %get-tuple-element.101), channel_id=1, source_target_pairs={{8,0},{16,8},{24,16},{9,1},{17,9},{25,17},{10,2},{18,10},{26,18},{... | collective-permute-start | bytes 24584 | tf_op jit(solution)/shard_map/ppermute | solution.py:25
  10.3 26.5 %collective-permute-start.1 = (f32[1,16,128]{2,1,0:T(8,128)S(1)}, f32[1,16,128]{2,1,0:T(8,128)S(1)}, u32[]{:S(2)}, u32[]{:S(2)}) collective-permute-start(f32[1,16,128]{2,1,0:T(8,128)S(1)} %get-tuple-element.100), channel_id=1, source_target_pairs={{0,8},{8,16},{16,24},{1,9},{9,17},{17,25},{2,10},{10,18},{18,26},{... | collective-permute-start | bytes 24584 | tf_op jit(solution)/shard_map/ppermute | solution.py:22
  26.6 22.5 %collective-permute-start.12 = (f32[1,8,64]{2,1,0:T(8,128)S(1)}, f32[1,8,64]{2,1,0:T(8,128)S(1)}, u32[]{:S(2)}, u32[]{:S(2)}) collective-permute-start(f32[1,8,64]{2,1,0:T(8,128)S(1)} %get-tuple-element.134), channel_id=1, source_target_pairs={{8,0},{16,8},{24,16},{9,1},{17,9},{25,17},{10,2},{18,10},{26,18},{... | collective-permute-start | bytes 6152 | tf_op jit(solution)/shard_map/ppermute | solution.py:25
  29.7 21.8 %collective-permute-start.13 = (f32[1,8,64]{2,1,0:T(8,128)S(1)}, f32[1,8,64]{2,1,0:T(8,128)S(1)}, u32[]{:S(2)}, u32[]{:S(2)}) collective-permute-start(f32[1,8,64]{2,1,0:T(8,128)S(1)} %get-tuple-element.133), channel_id=1, source_target_pairs={{0,8},{8,16},{16,24},{1,9},{9,17},{17,25},{2,10},{10,18},{18,26},{... | collective-permute-start | bytes 6152 | tf_op jit(solution)/shard_map/ppermute | solution.py:22
  32.9 99.8 %collective-permute-start.24 = (f32[1,4,32]{2,1,0:T(4,128)S(1)}, f32[1,4,32]{2,1,0:T(4,128)S(1)}, u32[]{:S(2)}, u32[]{:S(2)}) collective-permute-start(f32[1,4,32]{2,1,0:T(4,128)S(1)} %get-tuple-element.163), channel_id=1, source_target_pairs={{8,0},{16,8},{24,16},{9,1},{17,9},{25,17},{10,2},{18,10},{26,18},{... | collective-permute-start | bytes 1544 | tf_op jit(solution)/shard_map/ppermute | solution.py:25
  36.9 5.9 %collective-permute-start.2 = (f32[18,1,128]{2,1,0:T(1,128)S(1)}, f32[18,1,128]{2,1,0:T(1,128)S(1)}, u32[]{:S(2)}, u32[]{:S(2)}) collective-permute-start(f32[18,1,128]{2,1,0:T(1,128)S(1)} %get-tuple-element.95), channel_id=1, source_target_pairs={{1,0},{2,1},{3,2},{4,3},{5,4},{6,5},{7,6},{9,8},{10,9},{11,10},{12... | collective-permute-start | bytes 27656 | tf_op jit(solution)/shard_map/ppermute | solution.py:25
  40.2 6.5 %collective-permute-start.3 = (f32[18,1,128]{2,1,0:T(1,128)S(1)}, f32[18,1,128]{2,1,0:T(1,128)S(1)}, u32[]{:S(2)}, u32[]{:S(2)}) collective-permute-start(f32[18,1,128]{2,1,0:T(1,128)S(1)} %get-tuple-element.94), channel_id=1, source_target_pairs={{0,1},{1,2},{2,3},{3,4},{4,5},{5,6},{6,7},{8,9},{9,10},{10,11},{11... | collective-permute-start | bytes 27656 | tf_op jit(solution)/shard_map/ppermute | solution.py:22
  42.7 93.9 %collective-permute-start.25 = (f32[1,4,32]{2,1,0:T(4,128)S(1)}, f32[1,4,32]{2,1,0:T(4,128)S(1)}, u32[]{:S(2)}, u32[]{:S(2)}) collective-permute-start(f32[1,4,32]{2,1,0:T(4,128)S(1)} %get-tuple-element.162), channel_id=1, source_target_pairs={{0,8},{8,16},{16,24},{1,9},{9,17},{17,25},{2,10},{10,18},{18,26},{... | collective-permute-start | bytes 1544 | tf_op jit(solution)/shard_map/ppermute | solution.py:22
  47.2 7.9 %collective-permute-start.4 = (f32[3,1,16,128]{3,2,1,0:T(8,128)S(1)}, f32[3,1,16,128]{3,2,1,0:T(8,128)S(1)}, u32[]{:S(2)}, u32[]{:S(2)}) collective-permute-start(f32[3,1,16,128]{3,2,1,0:T(8,128)S(1)} %get-tuple-element.91), channel_id=1, source_target_pairs={{8,0},{16,8},{24,16},{9,1},{17,9},{25,17},{10,2},{18,10},{26,18},{... | collective-permute-start | bytes 73736 | tf_op jit(solution)/shard_map/ppermute | solution.py:25
  49.1 6.0 %collective-permute-start.5 = (f32[3,1,16,128]{3,2,1,0:T(8,128)S(1)}, f32[3,1,16,128]{3,2,1,0:T(8,128)S(1)}, u32[]{:S(2)}, u32[]{:S(2)}) collective-permute-start(f32[3,1,16,128]{3,2,1,0:T(8,128)S(1)} %get-tuple-element.90), channel_id=1, source_target_pairs={{0,8},{8,16},{16,24},{1,9},{9,17},{17,25},{2,10},{10,18},{18,26},{... | collective-permute-start | bytes 73736 | tf_op jit(solution)/shard_map/ppermute | solution.py:22
  51.5 16.6 %collective-permute-start.14 = (f32[10,1,64]{2,1,0:T(1,128)S(1)}, f32[10,1,64]{2,1,0:T(1,128)S(1)}, u32[]{:S(2)}, u32[]{:S(2)}) collective-permute-start(f32[10,1,64]{2,1,0:T(1,128)S(1)} %get-tuple-element.121), channel_id=1, source_target_pairs={{1,0},{2,1},{3,2},{4,3},{5,4},{6,5},{7,6},{9,8},{10,9},{11,10},{12... | collective-permute-start | bytes 7688 | tf_op jit(solution)/shard_map/ppermute | solution.py:25
  55.1 6.0 %collective-permute-start.6 = (f32[3,18,1,128]{3,2,1,0:T(1,128)S(1)}, f32[3,18,1,128]{3,2,1,0:T(1,128)S(1)}, u32[]{:S(2)}, u32[]{:S(2)}) collective-permute-start(f32[3,18,1,128]{3,2,1,0:T(1,128)S(1)} %get-tuple-element.81), channel_id=1, source_target_pairs={{1,0},{2,1},{3,2},{4,3},{5,4},{6,5},{7,6},{9,8},{10,9},{11,10},{12... | collective-permute-start | bytes 82952 | tf_op jit(solution)/shard_map/ppermute | solution.py:25
  58.3 6.7 %collective-permute-start.7 = (f32[3,18,1,128]{3,2,1,0:T(1,128)S(1)}, f32[3,18,1,128]{3,2,1,0:T(1,128)S(1)}, u32[]{:S(2)}, u32[]{:S(2)}) collective-permute-start(f32[3,18,1,128]{3,2,1,0:T(1,128)S(1)} %get-tuple-element.80), channel_id=1, source_target_pairs={{0,1},{1,2},{2,3},{3,4},{4,5},{5,6},{6,7},{8,9},{9,10},{10,11},{11... | collective-permute-start | bytes 82952 | tf_op jit(solution)/shard_map/ppermute | solution.py:22
  61.1 9.4 %collective-permute-start.15 = (f32[10,1,64]{2,1,0:T(1,128)S(1)}, f32[10,1,64]{2,1,0:T(1,128)S(1)}, u32[]{:S(2)}, u32[]{:S(2)}) collective-permute-start(f32[10,1,64]{2,1,0:T(1,128)S(1)} %get-tuple-element.120), channel_id=1, source_target_pairs={{0,1},{1,2},{2,3},{3,4},{4,5},{5,6},{6,7},{8,9},{9,10},{10,11},{11... | collective-permute-start | bytes 7688 | tf_op jit(solution)/shard_map/ppermute | solution.py:22
  68.1 5.1 %collective-permute-start.9 = (f32[3,1,16,128]{3,2,1,0:T(8,128)S(1)}, f32[3,1,16,128]{3,2,1,0:T(8,128)S(1)}, u32[]{:S(2)}, u32[]{:S(2)}) collective-permute-start(f32[3,1,16,128]{3,2,1,0:T(8,128)S(1)} %get-tuple-element.88), channel_id=1, source_target_pairs={{0,8},{8,16},{16,24},{1,9},{9,17},{17,25},{2,10},{10,18},{18,26},{... | collective-permute-start | bytes 73736 | tf_op jit(solution)/shard_map/ppermute | solution.py:22
  73.3 6.0 %collective-permute-start.10 = (f32[3,18,1,128]{3,2,1,0:T(1,128)S(1)}, f32[3,18,1,128]{3,2,1,0:T(1,128)S(1)}, u32[]{:S(2)}, u32[]{:S(2)}) collective-permute-start(f32[3,18,1,128]{3,2,1,0:T(1,128)S(1)} %get-tuple-element.79), channel_id=1, source_target_pairs={{1,0},{2,1},{3,2},{4,3},{5,4},{6,5},{7,6},{9,8},{10,9},{11,10},{12... | collective-permute-start | bytes 82952 | tf_op jit(solution)/shard_map/ppermute | solution.py:25
  76.8 6.7 %collective-permute-start.11 = (f32[3,18,1,128]{3,2,1,0:T(1,128)S(1)}, f32[3,18,1,128]{3,2,1,0:T(1,128)S(1)}, u32[]{:S(2)}, u32[]{:S(2)}) collective-permute-start(f32[3,18,1,128]{3,2,1,0:T(1,128)S(1)} %get-tuple-element.78), channel_id=1, source_target_pairs={{0,1},{1,2},{2,3},{3,4},{4,5},{5,6},{6,7},{8,9},{9,10},{10,11},{11... | collective-permute-start | bytes 82952 | tf_op jit(solution)/shard_map/ppermute | solution.py:22
  120.7 8.1 %collective-permute-start.16 = (f32[3,1,8,64]{3,2,1,0:T(8,128)S(1)}, f32[3,1,8,64]{3,2,1,0:T(8,128)S(1)}, u32[]{:S(2)}, u32[]{:S(2)}) collective-permute-start(f32[3,1,8,64]{3,2,1,0:T(8,128)S(1)} %get-tuple-element.119), channel_id=1, source_target_pairs={{8,0},{16,8},{24,16},{9,1},{17,9},{25,17},{10,2},{18,10},{26,18},{... | collective-permute-start | bytes 18440 | tf_op jit(solution)/shard_map/ppermute | solution.py:25
  122.7 8.1 %collective-permute-start.17 = (f32[3,1,8,64]{3,2,1,0:T(8,128)S(1)}, f32[3,1,8,64]{3,2,1,0:T(8,128)S(1)}, u32[]{:S(2)}, u32[]{:S(2)}) collective-permute-start(f32[3,1,8,64]{3,2,1,0:T(8,128)S(1)} %get-tuple-element.118), channel_id=1, source_target_pairs={{0,8},{8,16},{16,24},{1,9},{9,17},{17,25},{2,10},{10,18},{18,26},{... | collective-permute-start | bytes 18440 | tf_op jit(solution)/shard_map/ppermute | solution.py:22
  125.7 46.6 %collective-permute-start.36 = (f32[1,2,16]{2,1,0:T(2,128)}, f32[1,2,16]{2,1,0:T(2,128)}, u32[]{:S(2)}, u32[]{:S(2)}) collective-permute-start(f32[1,2,16]{2,1,0:T(2,128)} %get-tuple-element.182), channel_id=1, source_target_pairs={{8,0},{16,8},{24,16},{9,1},{17,9},{25,17},{10,2},{18,10},{26,18},{... | collective-permute-start | bytes 392 | tf_op jit(solution)/shard_map/ppermute | solution.py:25
  128.8 43.5 %collective-permute-start.37 = (f32[1,2,16]{2,1,0:T(2,128)}, f32[1,2,16]{2,1,0:T(2,128)}, u32[]{:S(2)}, u32[]{:S(2)}) collective-permute-start(f32[1,2,16]{2,1,0:T(2,128)} %get-tuple-element.181), channel_id=1, source_target_pairs={{0,8},{8,16},{16,24},{1,9},{9,17},{17,25},{2,10},{10,18},{18,26},{... | collective-permute-start | bytes 392 | tf_op jit(solution)/shard_map/ppermute | solution.py:22
  130.8 8.7 %collective-permute-start.18 = (f32[3,10,1,64]{3,2,1,0:T(1,128)S(1)}, f32[3,10,1,64]{3,2,1,0:T(1,128)S(1)}, u32[]{:S(2)}, u32[]{:S(2)}) collective-permute-start(f32[3,10,1,64]{3,2,1,0:T(1,128)S(1)} %get-tuple-element.109), channel_id=1, source_target_pairs={{1,0},{2,1},{3,2},{4,3},{5,4},{6,5},{7,6},{9,8},{10,9},{11,10},{12... | collective-permute-start | bytes 23048 | tf_op jit(solution)/shard_map/ppermute | solution.py:25
  132.8 9.8 %collective-permute-start.19 = (f32[3,10,1,64]{3,2,1,0:T(1,128)S(1)}, f32[3,10,1,64]{3,2,1,0:T(1,128)S(1)}, u32[]{:S(2)}, u32[]{:S(2)}) collective-permute-start(f32[3,10,1,64]{3,2,1,0:T(1,128)S(1)} %get-tuple-element.108), channel_id=1, source_target_pairs={{0,1},{1,2},{2,3},{3,4},{4,5},{5,6},{6,7},{8,9},{9,10},{10,11},{11... | collective-permute-start | bytes 23048 | tf_op jit(solution)/shard_map/ppermute | solution.py:22
  136.7 8.8 %collective-permute-start.26 = (f32[6,1,32]{2,1,0:T(1,128)S(1)}, f32[6,1,32]{2,1,0:T(1,128)S(1)}, u32[]{:S(2)}, u32[]{:S(2)}) collective-permute-start(f32[6,1,32]{2,1,0:T(1,128)S(1)} %get-tuple-element.158), channel_id=1, source_target_pairs={{1,0},{2,1},{3,2},{4,3},{5,4},{6,5},{7,6},{9,8},{10,9},{11,10},{12... | collective-permute-start | bytes 2312 | tf_op jit(solution)/shard_map/ppermute | solution.py:25
  139.6 7.9 %collective-permute-start.27 = (f32[6,1,32]{2,1,0:T(1,128)S(1)}, f32[6,1,32]{2,1,0:T(1,128)S(1)}, u32[]{:S(2)}, u32[]{:S(2)}) collective-permute-start(f32[6,1,32]{2,1,0:T(1,128)S(1)} %get-tuple-element.157), channel_id=1, source_target_pairs={{0,1},{1,2},{2,3},{3,4},{4,5},{5,6},{6,7},{8,9},{9,10},{10,11},{11... | collective-permute-start | bytes 2312 | tf_op jit(solution)/shard_map/ppermute | solution.py:22
  150.6 6.8 %collective-permute-start.22 = (f32[3,10,1,64]{3,2,1,0:T(1,128)S(1)}, f32[3,10,1,64]{3,2,1,0:T(1,128)S(1)}, u32[]{:S(2)}, u32[]{:S(2)}) collective-permute-start(f32[3,10,1,64]{3,2,1,0:T(1,128)S(1)} %get-tuple-element.107), channel_id=1, source_target_pairs={{1,0},{2,1},{3,2},{4,3},{5,4},{6,5},{7,6},{9,8},{10,9},{11,10},{12... | collective-permute-start | bytes 23048 | tf_op jit(solution)/shard_map/ppermute | solution.py:25
  154.6 6.5 %collective-permute-start.23 = (f32[3,10,1,64]{3,2,1,0:T(1,128)S(1)}, f32[3,10,1,64]{3,2,1,0:T(1,128)S(1)}, u32[]{:S(2)}, u32[]{:S(2)}) collective-permute-start(f32[3,10,1,64]{3,2,1,0:T(1,128)S(1)} %get-tuple-element.106), channel_id=1, source_target_pairs={{0,1},{1,2},{2,3},{3,4},{4,5},{5,6},{6,7},{8,9},{9,10},{10,11},{11... | collective-permute-start | bytes 23048 | tf_op jit(solution)/shard_map/ppermute | solution.py:22
  174.9 11.7 %collective-permute-start.30 = (f32[3,6,1,32]{3,2,1,0:T(1,128)S(1)}, f32[3,6,1,32]{3,2,1,0:T(1,128)S(1)}, u32[]{:S(2)}, u32[]{:S(2)}) collective-permute-start(f32[3,6,1,32]{3,2,1,0:T(1,128)S(1)} %get-tuple-element.129), channel_id=1, source_target_pairs={{1,0},{2,1},{3,2},{4,3},{5,4},{6,5},{7,6},{9,8},{10,9},{11,10},{12... | collective-permute-start | bytes 6920 | tf_op jit(solution)/shard_map/ppermute | solution.py:25
  176.8 9.8 %collective-permute-start.31 = (f32[3,6,1,32]{3,2,1,0:T(1,128)S(1)}, f32[3,6,1,32]{3,2,1,0:T(1,128)S(1)}, u32[]{:S(2)}, u32[]{:S(2)}) collective-permute-start(f32[3,6,1,32]{3,2,1,0:T(1,128)S(1)} %get-tuple-element.128), channel_id=1, source_target_pairs={{0,1},{1,2},{2,3},{3,4},{4,5},{5,6},{6,7},{8,9},{9,10},{10,11},{11... | collective-permute-start | bytes 6920 | tf_op jit(solution)/shard_map/ppermute | solution.py:22
  180.8 11.3 %collective-permute-start.38 = (f32[4,1,16]{2,1,0:T(1,128)S(1)}, f32[4,1,16]{2,1,0:T(1,128)S(1)}, u32[]{:S(2)}, u32[]{:S(2)}) collective-permute-start(f32[4,1,16]{2,1,0:T(1,128)S(1)} %get-tuple-element.179), channel_id=1, source_target_pairs={{1,0},{2,1},{3,2},{4,3},{5,4},{6,5},{7,6},{9,8},{10,9},{11,10},{12... | collective-permute-start | bytes 776 | tf_op jit(solution)/shard_map/ppermute | solution.py:25
  183.6 8.5 %collective-permute-start.39 = (f32[4,1,16]{2,1,0:T(1,128)S(1)}, f32[4,1,16]{2,1,0:T(1,128)S(1)}, u32[]{:S(2)}, u32[]{:S(2)}) collective-permute-start(f32[4,1,16]{2,1,0:T(1,128)S(1)} %get-tuple-element.178), channel_id=1, source_target_pairs={{0,1},{1,2},{2,3},{3,4},{4,5},{5,6},{6,7},{8,9},{9,10},{10,11},{11... | collective-permute-start | bytes 776 | tf_op jit(solution)/shard_map/ppermute | solution.py:22
  194.6 6.7 %collective-permute-start.34 = (f32[3,6,1,32]{3,2,1,0:T(1,128)S(1)}, f32[3,6,1,32]{3,2,1,0:T(1,128)S(1)}, u32[]{:S(2)}, u32[]{:S(2)}) collective-permute-start(f32[3,6,1,32]{3,2,1,0:T(1,128)S(1)} %get-tuple-element.127), channel_id=1, source_target_pairs={{1,0},{2,1},{3,2},{4,3},{5,4},{6,5},{7,6},{9,8},{10,9},{11,10},{12... | collective-permute-start | bytes 6920 | tf_op jit(solution)/shard_map/ppermute | solution.py:25
  198.4 6.5 %collective-permute-start.35 = (f32[3,6,1,32]{3,2,1,0:T(1,128)S(1)}, f32[3,6,1,32]{3,2,1,0:T(1,128)S(1)}, u32[]{:S(2)}, u32[]{:S(2)}) collective-permute-start(f32[3,6,1,32]{3,2,1,0:T(1,128)S(1)} %get-tuple-element.126), channel_id=1, source_target_pairs={{0,1},{1,2},{2,3},{3,4},{4,5},{5,6},{6,7},{8,9},{9,10},{10,11},{11... | collective-permute-start | bytes 6920 | tf_op jit(solution)/shard_map/ppermute | solution.py:22
  213.2 5.9 %collective-permute-start.42 = (f32[3,4,1,16]{3,2,1,0:T(1,128)S(1)}, f32[3,4,1,16]{3,2,1,0:T(1,128)S(1)}, u32[]{:S(2)}, u32[]{:S(2)}) collective-permute-start(f32[3,4,1,16]{3,2,1,0:T(1,128)S(1)} %get-tuple-element.156), channel_id=1, source_target_pairs={{1,0},{2,1},{3,2},{4,3},{5,4},{6,5},{7,6},{9,8},{10,9},{11,10},{12... | collective-permute-start | bytes 2312 | tf_op jit(solution)/shard_map/ppermute | solution.py:25
  215.1 6.4 %collective-permute-start.43 = (f32[3,4,1,16]{3,2,1,0:T(1,128)S(1)}, f32[3,4,1,16]{3,2,1,0:T(1,128)S(1)}, u32[]{:S(2)}, u32[]{:S(2)}) collective-permute-start(f32[3,4,1,16]{3,2,1,0:T(1,128)S(1)} %get-tuple-element.155), channel_id=1, source_target_pairs={{0,1},{1,2},{2,3},{3,4},{4,5},{5,6},{6,7},{8,9},{9,10},{10,11},{11... | collective-permute-start | bytes 2312 | tf_op jit(solution)/shard_map/ppermute | solution.py:22
  228.6 5.9 %collective-permute-start.46 = (f32[3,4,1,16]{3,2,1,0:T(1,128)S(1)}, f32[3,4,1,16]{3,2,1,0:T(1,128)S(1)}, u32[]{:S(2)}, u32[]{:S(2)}) collective-permute-start(f32[3,4,1,16]{3,2,1,0:T(1,128)S(1)} %get-tuple-element.154), channel_id=1, source_target_pairs={{1,0},{2,1},{3,2},{4,3},{5,4},{6,5},{7,6},{9,8},{10,9},{11,10},{12... | collective-permute-start | bytes 2312 | tf_op jit(solution)/shard_map/ppermute | solution.py:25
  231.5 6.4 %collective-permute-start.47 = (f32[3,4,1,16]{3,2,1,0:T(1,128)S(1)}, f32[3,4,1,16]{3,2,1,0:T(1,128)S(1)}, u32[]{:S(2)}, u32[]{:S(2)}) collective-permute-start(f32[3,4,1,16]{3,2,1,0:T(1,128)S(1)} %get-tuple-element.153), channel_id=1, source_target_pairs={{0,1},{1,2},{2,3},{3,4},{4,5},{5,6},{6,7},{8,9},{9,10},{10,11},{11... | collective-permute-start | bytes 2312 | tf_op jit(solution)/shard_map/ppermute | solution.py:22
  245.1 5.9 %collective-permute-start.50 = (f32[3,4,1,16]{3,2,1,0:T(1,128)S(1)}, f32[3,4,1,16]{3,2,1,0:T(1,128)S(1)}, u32[]{:S(2)}, u32[]{:S(2)}) collective-permute-start(f32[3,4,1,16]{3,2,1,0:T(1,128)S(1)} %get-tuple-element.152), channel_id=1, source_target_pairs={{1,0},{2,1},{3,2},{4,3},{5,4},{6,5},{7,6},{9,8},{10,9},{11,10},{12... | collective-permute-start | bytes 2312 | tf_op jit(solution)/shard_map/ppermute | solution.py:25
  247.0 6.4 %collective-permute-start.51 = (f32[3,4,1,16]{3,2,1,0:T(1,128)S(1)}, f32[3,4,1,16]{3,2,1,0:T(1,128)S(1)}, u32[]{:S(2)}, u32[]{:S(2)}) collective-permute-start(f32[3,4,1,16]{3,2,1,0:T(1,128)S(1)} %get-tuple-element.151), channel_id=1, source_target_pairs={{0,1},{1,2},{2,3},{3,4},{4,5},{5,6},{6,7},{8,9},{9,10},{10,11},{11... | collective-permute-start | bytes 2312 | tf_op jit(solution)/shard_map/ppermute | solution.py:22
  260.5 5.9 %collective-permute-start.54 = (f32[3,4,1,16]{3,2,1,0:T(1,128)S(1)}, f32[3,4,1,16]{3,2,1,0:T(1,128)S(1)}, u32[]{:S(2)}, u32[]{:S(2)}) collective-permute-start(f32[3,4,1,16]{3,2,1,0:T(1,128)S(1)} %get-tuple-element.150), channel_id=1, source_target_pairs={{1,0},{2,1},{3,2},{4,3},{5,4},{6,5},{7,6},{9,8},{10,9},{11,10},{12... | collective-permute-start | bytes 2312 | tf_op jit(solution)/shard_map/ppermute | solution.py:25
  263.4 6.4 %collective-permute-start.55 = (f32[3,4,1,16]{3,2,1,0:T(1,128)S(1)}, f32[3,4,1,16]{3,2,1,0:T(1,128)S(1)}, u32[]{:S(2)}, u32[]{:S(2)}) collective-permute-start(f32[3,4,1,16]{3,2,1,0:T(1,128)S(1)} %get-tuple-element.149), channel_id=1, source_target_pairs={{0,1},{1,2},{2,3},{3,4},{4,5},{5,6},{6,7},{8,9},{9,10},{10,11},{11... | collective-permute-start | bytes 2312 | tf_op jit(solution)/shard_map/ppermute | solution.py:22
  276.9 5.9 %collective-permute-start.58 = (f32[3,4,1,16]{3,2,1,0:T(1,128)S(1)}, f32[3,4,1,16]{3,2,1,0:T(1,128)S(1)}, u32[]{:S(2)}, u32[]{:S(2)}) collective-permute-start(f32[3,4,1,16]{3,2,1,0:T(1,128)S(1)} %get-tuple-element.148), channel_id=1, source_target_pairs={{1,0},{2,1},{3,2},{4,3},{5,4},{6,5},{7,6},{9,8},{10,9},{11,10},{12... | collective-permute-start | bytes 2312 | tf_op jit(solution)/shard_map/ppermute | solution.py:25
  278.9 6.4 %collective-permute-start.59 = (f32[3,4,1,16]{3,2,1,0:T(1,128)S(1)}, f32[3,4,1,16]{3,2,1,0:T(1,128)S(1)}, u32[]{:S(2)}, u32[]{:S(2)}) collective-permute-start(f32[3,4,1,16]{3,2,1,0:T(1,128)S(1)} %get-tuple-element.147), channel_id=1, source_target_pairs={{0,1},{1,2},{2,3},{3,4},{4,5},{5,6},{6,7},{8,9},{9,10},{10,11},{11... | collective-permute-start | bytes 2312 | tf_op jit(solution)/shard_map/ppermute | solution.py:22
  292.4 5.9 %collective-permute-start.62 = (f32[3,4,1,16]{3,2,1,0:T(1,128)S(1)}, f32[3,4,1,16]{3,2,1,0:T(1,128)S(1)}, u32[]{:S(2)}, u32[]{:S(2)}) collective-permute-start(f32[3,4,1,16]{3,2,1,0:T(1,128)S(1)} %get-tuple-element.146), channel_id=1, source_target_pairs={{1,0},{2,1},{3,2},{4,3},{5,4},{6,5},{7,6},{9,8},{10,9},{11,10},{12... | collective-permute-start | bytes 2312 | tf_op jit(solution)/shard_map/ppermute | solution.py:25
  294.3 6.4 %collective-permute-start.63 = (f32[3,4,1,16]{3,2,1,0:T(1,128)S(1)}, f32[3,4,1,16]{3,2,1,0:T(1,128)S(1)}, u32[]{:S(2)}, u32[]{:S(2)}) collective-permute-start(f32[3,4,1,16]{3,2,1,0:T(1,128)S(1)} %get-tuple-element.145), channel_id=1, source_target_pairs={{0,1},{1,2},{2,3},{3,4},{4,5},{5,6},{6,7},{8,9},{9,10},{10,11},{11... | collective-permute-start | bytes 2312 | tf_op jit(solution)/shard_map/ppermute | solution.py:22
  307.8 5.9 %collective-permute-start.66 = (f32[3,4,1,16]{3,2,1,0:T(1,128)S(1)}, f32[3,4,1,16]{3,2,1,0:T(1,128)S(1)}, u32[]{:S(2)}, u32[]{:S(2)}) collective-permute-start(f32[3,4,1,16]{3,2,1,0:T(1,128)S(1)} %get-tuple-element.144), channel_id=1, source_target_pairs={{1,0},{2,1},{3,2},{4,3},{5,4},{6,5},{7,6},{9,8},{10,9},{11,10},{12... | collective-permute-start | bytes 2312 | tf_op jit(solution)/shard_map/ppermute | solution.py:25
  309.8 6.4 %collective-permute-start.67 = (f32[3,4,1,16]{3,2,1,0:T(1,128)S(1)}, f32[3,4,1,16]{3,2,1,0:T(1,128)S(1)}, u32[]{:S(2)}, u32[]{:S(2)}) collective-permute-start(f32[3,4,1,16]{3,2,1,0:T(1,128)S(1)} %get-tuple-element.143), channel_id=1, source_target_pairs={{0,1},{1,2},{2,3},{3,4},{4,5},{5,6},{6,7},{8,9},{9,10},{10,11},{11... | collective-permute-start | bytes 2312 | tf_op jit(solution)/shard_map/ppermute | solution.py:22
  323.8 5.9 %collective-permute-start.70 = (f32[3,6,1,32]{3,2,1,0:T(1,128)S(1)}, f32[3,6,1,32]{3,2,1,0:T(1,128)S(1)}, u32[]{:S(2)}, u32[]{:S(2)}) collective-permute-start(f32[3,6,1,32]{3,2,1,0:T(1,128)S(1)} %get-tuple-element.125), channel_id=1, source_target_pairs={{1,0},{2,1},{3,2},{4,3},{5,4},{6,5},{7,6},{9,8},{10,9},{11,10},{12... | collective-permute-start | bytes 6920 | tf_op jit(solution)/shard_map/ppermute | solution.py:25
  325.7 6.5 %collective-permute-start.71 = (f32[3,6,1,32]{3,2,1,0:T(1,128)S(1)}, f32[3,6,1,32]{3,2,1,0:T(1,128)S(1)}, u32[]{:S(2)}, u32[]{:S(2)}) collective-permute-start(f32[3,6,1,32]{3,2,1,0:T(1,128)S(1)} %get-tuple-element.124), channel_id=1, source_target_pairs={{0,1},{1,2},{2,3},{3,4},{4,5},{5,6},{6,7},{8,9},{9,10},{10,11},{11... | collective-permute-start | bytes 6920 | tf_op jit(solution)/shard_map/ppermute | solution.py:22
  339.4 5.9 %collective-permute-start.74 = (f32[3,6,1,32]{3,2,1,0:T(1,128)S(1)}, f32[3,6,1,32]{3,2,1,0:T(1,128)S(1)}, u32[]{:S(2)}, u32[]{:S(2)}) collective-permute-start(f32[3,6,1,32]{3,2,1,0:T(1,128)S(1)} %get-tuple-element.123), channel_id=1, source_target_pairs={{1,0},{2,1},{3,2},{4,3},{5,4},{6,5},{7,6},{9,8},{10,9},{11,10},{12... | collective-permute-start | bytes 6920 | tf_op jit(solution)/shard_map/ppermute | solution.py:25
  341.3 6.5 %collective-permute-start.75 = (f32[3,6,1,32]{3,2,1,0:T(1,128)S(1)}, f32[3,6,1,32]{3,2,1,0:T(1,128)S(1)}, u32[]{:S(2)}, u32[]{:S(2)}) collective-permute-start(f32[3,6,1,32]{3,2,1,0:T(1,128)S(1)} %get-tuple-element.122), channel_id=1, source_target_pairs={{0,1},{1,2},{2,3},{3,4},{4,5},{5,6},{6,7},{8,9},{9,10},{10,11},{11... | collective-permute-start | bytes 6920 | tf_op jit(solution)/shard_map/ppermute | solution.py:22
  355.9 5.9 %collective-permute-start.78 = (f32[3,10,1,64]{3,2,1,0:T(1,128)S(1)}, f32[3,10,1,64]{3,2,1,0:T(1,128)S(1)}, u32[]{:S(2)}, u32[]{:S(2)}) collective-permute-start(f32[3,10,1,64]{3,2,1,0:T(1,128)S(1)} %get-tuple-element.105), channel_id=1, source_target_pairs={{1,0},{2,1},{3,2},{4,3},{5,4},{6,5},{7,6},{9,8},{10,9},{11,10},{12... | collective-permute-start | bytes 23048 | tf_op jit(solution)/shard_map/ppermute | solution.py:25
  357.8 6.5 %collective-permute-start.79 = (f32[3,10,1,64]{3,2,1,0:T(1,128)S(1)}, f32[3,10,1,64]{3,2,1,0:T(1,128)S(1)}, u32[]{:S(2)}, u32[]{:S(2)}) collective-permute-start(f32[3,10,1,64]{3,2,1,0:T(1,128)S(1)} %get-tuple-element.104), channel_id=1, source_target_pairs={{0,1},{1,2},{2,3},{3,4},{4,5},{5,6},{6,7},{8,9},{9,10},{10,11},{11... | collective-permute-start | bytes 23048 | tf_op jit(solution)/shard_map/ppermute | solution.py:22
  371.8 5.9 %collective-permute-start.82 = (f32[3,10,1,64]{3,2,1,0:T(1,128)S(1)}, f32[3,10,1,64]{3,2,1,0:T(1,128)S(1)}, u32[]{:S(2)}, u32[]{:S(2)}) collective-permute-start(f32[3,10,1,64]{3,2,1,0:T(1,128)S(1)} %get-tuple-element.103), channel_id=1, source_target_pairs={{1,0},{2,1},{3,2},{4,3},{5,4},{6,5},{7,6},{9,8},{10,9},{11,10},{12... | collective-permute-start | bytes 23048 | tf_op jit(solution)/shard_map/ppermute | solution.py:25
  373.7 6.5 %collective-permute-start.83 = (f32[3,10,1,64]{3,2,1,0:T(1,128)S(1)}, f32[3,10,1,64]{3,2,1,0:T(1,128)S(1)}, u32[]{:S(2)}, u32[]{:S(2)}) collective-permute-start(f32[3,10,1,64]{3,2,1,0:T(1,128)S(1)} %get-tuple-element.102), channel_id=1, source_target_pairs={{0,1},{1,2},{2,3},{3,4},{4,5},{5,6},{6,7},{8,9},{9,10},{10,11},{11... | collective-permute-start | bytes 23048 | tf_op jit(solution)/shard_map/ppermute | solution.py:22
  389.4 5.1 %collective-permute-start.85 = (f32[3,1,16,128]{3,2,1,0:T(8,128)S(1)}, f32[3,1,16,128]{3,2,1,0:T(8,128)S(1)}, u32[]{:S(2)}, u32[]{:S(2)}) collective-permute-start(f32[3,1,16,128]{3,2,1,0:T(8,128)S(1)} %get-tuple-element.86), channel_id=1, source_target_pairs={{0,8},{8,16},{16,24},{1,9},{9,17},{17,25},{2,10},{10,18},{18,26},{... | collective-permute-start | bytes 73736 | tf_op jit(solution)/shard_map/ppermute | solution.py:22
  394.6 6.1 %collective-permute-start.86 = (f32[3,18,1,128]{3,2,1,0:T(1,128)S(1)}, f32[3,18,1,128]{3,2,1,0:T(1,128)S(1)}, u32[]{:S(2)}, u32[]{:S(2)}) collective-permute-start(f32[3,18,1,128]{3,2,1,0:T(1,128)S(1)} %get-tuple-element.77), channel_id=1, source_target_pairs={{1,0},{2,1},{3,2},{4,3},{5,4},{6,5},{7,6},{9,8},{10,9},{11,10},{12... | collective-permute-start | bytes 82952 | tf_op jit(solution)/shard_map/ppermute | solution.py:25
  396.5 6.7 %collective-permute-start.87 = (f32[3,18,1,128]{3,2,1,0:T(1,128)S(1)}, f32[3,18,1,128]{3,2,1,0:T(1,128)S(1)}, u32[]{:S(2)}, u32[]{:S(2)}) collective-permute-start(f32[3,18,1,128]{3,2,1,0:T(1,128)S(1)} %get-tuple-element.76), channel_id=1, source_target_pairs={{0,1},{1,2},{2,3},{3,4},{4,5},{5,6},{6,7},{8,9},{9,10},{10,11},{11... | collective-permute-start | bytes 82952 | tf_op jit(solution)/shard_map/ppermute | solution.py:22
  406.4 5.1 %collective-permute-start.89 = (f32[3,1,16,128]{3,2,1,0:T(8,128)S(1)}, f32[3,1,16,128]{3,2,1,0:T(8,128)S(1)}, u32[]{:S(2)}, u32[]{:S(2)}) collective-permute-start(f32[3,1,16,128]{3,2,1,0:T(8,128)S(1)} %get-tuple-element.84), channel_id=1, source_target_pairs={{0,8},{8,16},{16,24},{1,9},{9,17},{17,25},{2,10},{10,18},{18,26},{... | collective-permute-start | bytes 73736 | tf_op jit(solution)/shard_map/ppermute | solution.py:22
  411.6 5.9 %collective-permute-start.90 = (f32[3,18,1,128]{3,2,1,0:T(1,128)S(1)}, f32[3,18,1,128]{3,2,1,0:T(1,128)S(1)}, u32[]{:S(2)}, u32[]{:S(2)}) collective-permute-start(f32[3,18,1,128]{3,2,1,0:T(1,128)S(1)} %get-tuple-element.75), channel_id=1, source_target_pairs={{1,0},{2,1},{3,2},{4,3},{5,4},{6,5},{7,6},{9,8},{10,9},{11,10},{12... | collective-permute-start | bytes 82952 | tf_op jit(solution)/shard_map/ppermute | solution.py:25
  413.5 6.7 %collective-permute-start.91 = (f32[3,18,1,128]{3,2,1,0:T(1,128)S(1)}, f32[3,18,1,128]{3,2,1,0:T(1,128)S(1)}, u32[]{:S(2)}, u32[]{:S(2)}) collective-permute-start(f32[3,18,1,128]{3,2,1,0:T(1,128)S(1)} %get-tuple-element.74), channel_id=1, source_target_pairs={{0,1},{1,2},{2,3},{3,4},{4,5},{5,6},{6,7},{8,9},{9,10},{10,11},{11... | collective-permute-start | bytes 82952 | tf_op jit(solution)/shard_map/ppermute | solution.py:22
  423.4 5.1 %collective-permute-start.93 = (f32[3,1,16,128]{3,2,1,0:T(8,128)S(1)}, f32[3,1,16,128]{3,2,1,0:T(8,128)S(1)}, u32[]{:S(2)}, u32[]{:S(2)}) collective-permute-start(f32[3,1,16,128]{3,2,1,0:T(8,128)S(1)} %get-tuple-element.82), channel_id=1, source_target_pairs={{0,8},{8,16},{16,24},{1,9},{9,17},{17,25},{2,10},{10,18},{18,26},{... | collective-permute-start | bytes 73736 | tf_op jit(solution)/shard_map/ppermute | solution.py:22
  428.6 5.9 %collective-permute-start.94 = (f32[3,18,1,128]{3,2,1,0:T(1,128)S(1)}, f32[3,18,1,128]{3,2,1,0:T(1,128)S(1)}, u32[]{:S(2)}, u32[]{:S(2)}) collective-permute-start(f32[3,18,1,128]{3,2,1,0:T(1,128)S(1)} %get-tuple-element.73), channel_id=1, source_target_pairs={{1,0},{2,1},{3,2},{4,3},{5,4},{6,5},{7,6},{9,8},{10,9},{11,10},{12... | collective-permute-start | bytes 82952 | tf_op jit(solution)/shard_map/ppermute | solution.py:25
  430.5 6.7 %collective-permute-start.95 = (f32[3,18,1,128]{3,2,1,0:T(1,128)S(1)}, f32[3,18,1,128]{3,2,1,0:T(1,128)S(1)}, u32[]{:S(2)}, u32[]{:S(2)}) collective-permute-start(f32[3,18,1,128]{3,2,1,0:T(1,128)S(1)} %get-tuple-element.72), channel_id=1, source_target_pairs={{0,1},{1,2},{2,3},{3,4},{4,5},{5,6},{6,7},{8,9},{9,10},{10,11},{11... | collective-permute-start | bytes 82952 | tf_op jit(solution)/shard_map/ppermute | solution.py:22
  (84 other events, 2594.1 us)
where the time goes:
time: 442 us; the launch traced here: 439 us
  starting transfers between devices  247 us (56%)
  waiting for transfers between devices  97.8 us (22%)
  local copies, waits for them, and re-layouts  51 us (12%)
  other arithmetic  39.8 us (9%)
    ppermute x48, starting transfers between devices, padded_2(): lax.ppermute(lax.slice_in_dim(block, block.shape[dim] - width, None, axis...  136 us
    ppermute x48, starting transfers between devices, padded_2(): lax.ppermute(lax.slice_in_dim(block, 0, width, axis=dim), axis, backward)  111 us
    ppermute x48, waiting for transfers between devices, padded_2(): lax.ppermute(lax.slice_in_dim(block, block.shape[dim] - width, None, axis...  97.7 us
    reshape x4, local copies, waits for them, and re-layouts, shrink(): blocks = arr.reshape(tuple(lead) + (za // 2, 2, yb // 2, 2, xc // 2, 2))  40.6 us
    reduce_sum x6, other arithmetic, shrink(): return blocks.mean(axis=(-5, -3, -1))  14.7 us
  transfers between devices with their start and end apart: 96, of which 37 were waited for; matrix products, arithmetic and copies ran while one was open for 15% of the time, Pallas kernels for 0%

commit v1 on v0

v1 whole, which is shorter than its diff:
```python
import jax
import jax.numpy as jnp
from jax import lax
from jax.experimental import pallas as pl
from jax.experimental.pallas import tpu as pltpu
from jax.sharding import PartitionSpec as P

OMEGA = 0.6
COUPLE = 0.05
CLASSES = 8
COARSE_SWEEPS = 8
LANES = 128
F32 = jnp.float32
DIRS = ((0, 1), (0, -1), (1, 0), (-1, 0), (1, 1), (1, -1), (-1, 1), (-1, -1))


class Grid:
    def __init__(self, nz, ny, oz, oy):
        self.nz, self.ny, self.oz, self.oy = nz, ny, oz, oy
        self.z, self.y = nz + 2 * oz, ny + 2 * oy
        self.rows = self.z * self.y

    def row(self, comp, z, y):
        return comp * self.rows + (z + self.oz) * self.y + y + self.oy

    def plane(self, comp, z):
        start = comp * self.rows + z * self.y
        if not isinstance(start, int):
            start = pl.multiple_of(start, 8)
        return pl.ds(start, self.y)


def segments(grid, dz, dy, depth):
    nz, ny = grid.nz, grid.ny

    def cell(step, d, n):
        return (n - step, -step) if d > 0 else (step - 1, n - 1 + step)

    out = []
    if dz == 0:
        for i in range(1, depth + 1):
            mine, there = cell(i, dy, ny)
            out.append((0, mine, 0, there, nz, True))
    elif dy == 0:
        for i in range(1, depth + 1):
            mine, there = cell(i, dz, nz)
            out.append((mine, 0, there, 0, ny, False))
    else:
        for i in range(1, depth):
            for j in range(1, depth + 1 - i):
                mz, tz = cell(i, dz, nz)
                my, ty = cell(j, dy, ny)
                out.append((mz, my, tz, ty, 1, False))
    return out


def message(grid, dz, dy, fields):
    out, at = [], 0
    for field, (comps, depth) in enumerate(fields):
        for comp in range(comps):
            for seg in segments(grid, dz, dy, depth):
                out.append((field, comp, seg, at))
                at += seg[4]
    return out, -(-at // 8) * 8


def window(grid, comp, z, y, count, along_z):
    start = grid.row(comp, z, y)
    if along_z:
        return pl.ds(start, count, stride=grid.y)
    return pl.ds(start, count)


class Exchange:
    def __init__(self, grid, fields, where, send, recv, ssem, rsem):
        self.grid, self.fields, self.where = grid, fields, where
        self.send, self.recv, self.ssem, self.rsem = send, recv, ssem, rsem

    def copy(self, d):
        dz, dy = DIRS[d]
        s, c, ns, nc = self.where
        target = (lax.rem(s + dz + ns, ns), lax.rem(c + dy + nc, nc))
        return pltpu.make_async_remote_copy(
            src_ref=self.send[d], dst_ref=self.recv[d], send_sem=self.ssem.at[d], recv_sem=self.rsem.at[d],
            device_id=target, device_id_type=pl.DeviceIdType.MESH)

    def exists(self, dz, dy):
        s, c, ns, nc = self.where
        ok = None
        for here, d, n in ((s, dz, ns), (c, dy, nc)):
            if d:
                near = here < n - 1 if d > 0 else here > 0
                ok = near if ok is None else jnp.logical_and(ok, near)
        return ok

    def start(self, refs):
        for d, (dz, dy) in enumerate(DIRS):
            rows, _ = message(self.grid, dz, dy, self.fields)

            @pl.when(self.exists(dz, dy))
            def _():
                for field, comp, (z, y, _, _, count, along), at in rows:
                    self.send[d][pl.ds(at, count), :] = refs[field][window(self.grid, comp, z, y, count, along), :]
                self.copy(d).start()

    def finish(self, refs):
        for d, (dz, dy) in enumerate(DIRS):
            rows, _ = message(self.grid, dz, dy, self.fields)

            @pl.when(self.exists(-dz, -dy))
            def _():
                self.copy(d).wait_recv()
                for field, comp, (_, _, z, y, count, along), at in rows:
                    refs[field][window(self.grid, comp, z, y, count, along), :] = self.recv[d][pl.ds(at, count), :]

    def drain(self):
        for d, (dz, dy) in enumerate(DIRS):
            @pl.when(self.exists(dz, dy))
            def _():
                self.copy(d).wait_send()


def lane_iota(rows):
    return lax.broadcasted_iota(jnp.int32, (rows, LANES), 1)


def right(v, step):
    return pltpu.roll(v, step % LANES, 1)


def left(v, step):
    return pltpu.roll(v, LANES - step, 1)


def down(v):
    return pltpu.roll(v, 1, 0)


def up(v):
    return pltpu.roll(v, v.shape[0] - 1, 0)


def pair_sum(v, step):
    lane = lane_iota(v.shape[0])
    first = lane % (2 * step) < step
    return v + jnp.where(first, left(v, step), right(v, step))


def rows_of(start, count):
    if not isinstance(start, int):
        start = pl.multiple_of(start, 8)
    return pl.ds(start, count)


class Level:
    def __init__(self, scale, xs, zs, group, ny, closed, plane, k, coef, size):
        self.scale, self.xs, self.zs, self.group, self.ny, self.closed = scale, xs, zs, group, ny, closed
        self.plane, self.k, self.coef, self.size = plane, k, coef, size

    def at(self, which, z):
        p = self.plane(0, z)
        return self.coef[which][p, :]

    def z_sides(self, get, z):
        after, before = get(z + 1), get(z - 1)
        if not self.group:
            return after, before
        here = get(z)
        lane = lane_iota(self.ny) % self.group
        turn = self.group - self.zs
        return (jnp.where(lane < turn, left(here, self.zs), right(after, turn)),
                jnp.where(lane >= self.zs, right(here, self.zs), left(before, turn)))

    def setup(self, low, high, mask):
        def body(z, carry):
            get = lambda i: self.k[self.plane(0, i), :]
            k = get(z)
            lane = lane_iota(self.ny)
            zp, zm = self.z_sides(get, z)
            inx = lane < LANES - self.xs
            inm = lane >= self.xs
            xp = jnp.where(inx, left(k, self.xs), 0.0)
            xm = jnp.where(inm, right(k, self.xs), 0.0)
            yp, ym = up(k), down(k)
            half = F32(0.5 * self.scale)
            if self.closed:
                row = lax.broadcasted_iota(jnp.int32, (self.ny, LANES), 0)
                iny, inw = row < self.ny - 1, row >= 1
                yp, ym = jnp.where(iny, yp, 0.0), jnp.where(inw, ym, 0.0)
            kzp, kzm = half * (k + zp), half * (k + zm)
            kyp, kym = half * (k + yp), half * (k + ym)
            kxp, kxm = half * (k + xp), half * (k + xm)
            total = kzp + kzm + kyp + kym + kxp + kxm
            if self.closed:
                kyp, kym = jnp.where(iny, kyp, 0.0), jnp.where(inw, kym, 0.0)
            kxp, kxm = jnp.where(inx, kxp, 0.0), jnp.where(inm, kxm, 0.0)
            inside = k > 0.0
            diag = jnp.where(inside, total + F32(2.0 * COUPLE) * k, 1.0)
            weight = jnp.where(inside, F32(OMEGA) / diag, 0.0)
            p = self.plane(0, z)
            if mask is not None:
                weight = weight * mask[p, :]
            for which, value in enumerate((kzp, kzm, kyp, kym, kxp, kxm, total + F32(COUPLE) * k, weight)):
                self.coef[which][p, :] = value
            return carry

        lax.fori_loop(low, high, body, 0)

    def first(self, low, high, rhs, out):
        def body(z, carry):
            weight = self.at(7, z)
            for c in range(3):
                p = self.plane(c, z)
                out[p, :] = weight * rhs[p, :]
            return carry

        lax.fori_loop(low, high, body, 0)

    def defect(self, z, u, rhs):
        kzp, kzm, kyp, kym, kxp, kxm, own = [self.at(i, z) for i in range(7)]
        couple = F32(COUPLE) * self.k[self.plane(0, z), :]
        field = [u[self.plane(c, z), :] for c in range(3)]
        shared = couple * (field[0] + field[1] + field[2])
        out = []
        for c in range(3):
            v = field[c]
            zp, zm = self.z_sides(lambda i: u[self.plane(c, i), :], z)
            near = (kzp * zp + kzm * zm) + (kyp * up(v) + kym * down(v))
            near = near + (kxp * left(v, self.xs) + kxm * right(v, self.xs))
            out.append((rhs[self.plane(c, z), :] - shared) + (near - own * v))
        return field, out

    def sweep(self, low, high, u, rhs, out, out_plane=None):
        place = out_plane or self.plane

        def body(z, carry):
            field, out_d = self.defect(z, u, rhs)
            weight = self.at(7, z)
            for c in range(3):
                out[place(c, z), :] = field[c] + weight * out_d[c]
            return carry

        lax.fori_loop(low, high, body, 0)

    def residual(self, low, high, u, rhs, mask, out):
        def body(z, carry):
            _, out_d = self.defect(z, u, rhs)
            for c in range(3):
                value = out_d[c]
                if mask is not None:
                    value = mask[self.plane(0, z), :] * value
                out(c, z, value)
            return carry

        lax.fori_loop(low, high, body, 0)


def kernel(ns, nc, g0, g1, ex, load, dens, moduli, fixed, out_u, out_r, *scratch):
    it = iter(scratch)
    take = lambda n: [next(it) for _ in range(n)]
    k0, m0, b0, ua, ub = take(5)
    c0 = take(8)
    k1, b1, va, vb = take(4)
    c1 = take(8)
    k2, b2, wa, wb, wf = take(5)
    c2 = take(8)
    k3, b3, xa, xb = take(4)
    c3 = take(8)
    pack, gather, stage = take(3)
    s, c = lax.axis_index("slab"), lax.axis_index("col")
    where = (s, c, ns, nc)
    rounds = []
    for grid, fields in ex:
        send, recv = take(8), take(8)
        ssem, rsem = take(2)
        rounds.append(Exchange(grid, fields, where, send, recv, ssem, rsem))
    gsend, grecv = take(2)
    ex_a, ex_k, ex_b, ex_u, ex_v = rounds
    n0, y0, n1, y1 = g0.nz, g0.ny, g1.nz, g1.ny

    def zero(ref):
        rows = ref.shape[0]
        ref[...] = jnp.zeros((rows, LANES), F32)

    for ref in (k0, m0, b0, k1):
        zero(ref)

    def fill(z, carry):
        src = pl.ds(pl.multiple_of(z * y0, 8), y0)
        d = dens[src, :]
        value = jnp.zeros((y0, LANES), F32)
        for klass in range(CLASSES):
            value = jnp.where(d == klass, moduli[klass], value)
        keep = 1.0 - fixed[src, :].astype(F32)
        wide = lambda v: jnp.concatenate(
            [jnp.zeros((g0.oy, LANES), F32), v, jnp.zeros((g0.oy, LANES), F32)], axis=0)
        k0[g0.plane(0, z + g0.oz), :] = wide(value)
        m0[g0.plane(0, z + g0.oz), :] = wide(keep)
        for comp in range(3):
            at = pl.ds(pl.multiple_of((comp * n0 + z) * y0, 8), y0)
            b0[g0.plane(comp, z + g0.oz), :] = wide(load[at, :])
        return carry

    lax.fori_loop(0, n0, fill, 0)
    ex_a.start([k0, m0, b0])

    def coarser(src, grid, comp, z, y, count, steps):
        total = None
        for dz in range(2):
            for dy in range(2):
                part = src[pl.ds(grid.row(comp, 2 * z + dz, 2 * y + dy), count, stride=2), :]
                total = part if total is None else total + part
        for step in steps:
            total = pair_sum(total, step)
        return total * F32(0.125)

    for z in range(n1):
        k1[pl.ds(g1.row(0, z, 0), y1), :] = coarser(k0, g0, 0, z, 0, y1, (1,))
    ex_k.start([k1])

    lane4 = lane_iota(4) % 4

    def packed(src, comp, slot):
        value = jnp.zeros((4, LANES), F32)
        for z in range(n1 // 2):
            value = jnp.where(lane4 == z, coarser(src, g1, comp, z, 0, y1 // 2, (2,)), value)
        pack[pl.ds(4 * slot, 4), :] = value

    packed(k1, 0, 3)
    for ref in (ua, ub, b1, va, vb):
        zero(ref)

    level0 = Level(1.0, 1, 0, 0, g0.y, False, g0.plane, k0, c0, g0.z)
    level1 = Level(0.25, 2, 0, 0, g1.y, False, g1.plane, k1, c1, g1.z)
    y2, y3 = 4 * nc, 2 * nc
    plane2 = lambda comp, z: rows_of((comp * (ns + 2) + z) * y2, y2)
    plane3 = lambda comp, z: rows_of((comp * (ns + 2) + z) * y3, y3)
    wide2 = lambda comp, z: rows_of((comp * (ns + 2) + z) * (y2 + 16) + 8, y2)
    level2 = Level(0.25**2, 4, 1, 4, y2, True, plane2, k2, c2, ns)
    level3 = Level(0.25**3, 8, 2, 4, y3, True, plane3, k3, c3, ns)
    for ref, comps, plane, rows in ((k2, 1, plane2, y2), (wa, 3, plane2, y2), (wb, 3, plane2, y2),
                                    (k3, 1, plane3, y3), (xa, 3, plane3, y3), (xb, 3, plane3, y3),
                                    (wf, 3, lambda comp, z: rows_of((comp * (ns + 2) + z) * (y2 + 16), y2 + 16), y2 + 16)):
        for comp in range(comps):
            for z in (0, ns + 1):
                ref[plane(comp, z), :] = jnp.zeros((rows, LANES), F32)

    ex_a.finish([k0, m0, b0])
    level0.setup(g0.oz - 2, g0.oz + n0 + 2, m0)
    level0.first(g0.oz - 2, g0.oz + n0 + 2, b0, ua)
    level0.sweep(g0.oz - 1, g0.oz + n0 + 1, ua, b0, ub)

    def keep0(comp, z, value):
        ua[g0.plane(comp, z), :] = value

    level0.residual(g0.oz, g0.oz + n0, ub, b0, m0, keep0)
    for comp in range(3):
        for z in range(n1):
            b1[pl.ds(g1.row(comp, z, 0), y1), :] = coarser(ua, g0, comp, z, 0, y1, (1,))
    ex_b.start([b1])
    ex_u.start([ub, m0])

    ex_k.finish([k1])
    level1.setup(g1.oz - 3, g1.oz + n1 + 3, None)
    ex_b.finish([b1])
    level1.first(g1.oz - 2, g1.oz + n1 + 2, b1, va)
    level1.sweep(g1.oz - 1, g1.oz + n1 + 1, va, b1, vb)

    def keep1(comp, z, value):
        va[g1.plane(comp, z), :] = value

    level1.residual(g1.oz, g1.oz + n1, vb, b1, None, keep1)
    for comp in range(3):
        packed(va, comp, comp)

    here = pl.ds(pl.multiple_of((s * nc + c) * 16, 16), 16)
    gather[here, :] = pack[...]

    def spread(t):
        target = (lax.rem(s + t // nc, ns), lax.rem(c + t % nc, nc))
        return pltpu.make_async_remote_copy(
            src_ref=gather.at[here], dst_ref=gather.at[here], send_sem=gsend.at[t], recv_sem=grecv.at[t],
            device_id=target, device_id_type=pl.DeviceIdType.MESH)

    def start_one(t, carry):
        spread(t).start()
        return carry

    lax.fori_loop(1, ns * nc, start_one, 0)
    ex_v.start([vb])

    def wait_one(t, carry):
        spread(t).wait_recv()
        return carry

    lax.fori_loop(1, ns * nc, wait_one, 0)

    def assemble(t, carry):
        z, pair = t // (nc // 2), t % (nc // 2)
        first = gather[pl.ds(pl.multiple_of(t * 32, 32), 16), :]
        second = gather[pl.ds(pl.multiple_of(t * 32 + 16, 16), 16), :]
        for f in range(4):
            value = jnp.concatenate([first[4 * f:4 * f + 4], second[4 * f:4 * f + 4]], axis=0)
            ref, comp = (k2, 0) if f == 3 else (b2, f)
            ref[pl.ds(pl.multiple_of((comp * (ns + 2) + z + 1) * y2 + pair * 8, 8), 8), :] = value
        return carry

    lax.fori_loop(0, ns * nc // 2, assemble, 0)
    level2.setup(1, ns + 1, None)
    level2.first(1, ns + 1, b2, wa)
    level2.sweep(1, ns + 1, wa, b2, wb)

    def keep2(comp, z, value):
        wa[plane2(comp, z), :] = value

    level2.residual(1, ns + 1, wb, b2, None, keep2)

    def shrink3(z, carry):
        for src, dst, comp in ((k2, k3, 0), (wa, b3, 0), (wa, b3, 1), (wa, b3, 2)):
            start = (comp * (ns + 2) + z) * y2
            total = src[pl.ds(start, y3, stride=2), :] + src[pl.ds(start + 1, y3, stride=2), :]
            dst[plane3(comp, z), :] = pair_sum(pair_sum(total, 1), 4) * F32(0.125)
        return carry

    lax.fori_loop(1, ns + 1, shrink3, 0)
    level3.setup(1, ns + 1, None)
    level3.first(1, ns + 1, b3, xa)
    old, new = xa, xb
    for turn in range(COARSE_SWEEPS - 1):
        level3.sweep(1, ns + 1, old, b3, new)
        old, new = new, old
    coarse = old

    def add2(z, carry):
        for comp in range(3):
            value = coarse[plane3(comp, z), :]
            stage[pl.ds(0, y3, stride=2), :] = value
            stage[pl.ds(1, y3, stride=2), :] = value
            p = plane2(comp, z)
            wb[p, :] = wb[p, :] + stage[pl.ds(0, y2), :]
        return carry

    lax.fori_loop(1, ns + 1, add2, 0)

    def clear(ref):
        for comp in range(3):
            for z in (0, ns + 1):
                ref[plane2(comp, z), :] = jnp.zeros((y2, LANES), F32)

    clear(wa)
    level2.sweep(1, ns + 1, wb, b2, wa)
    level2.sweep(1, ns + 1, wa, b2, wf, wide2)

    ex_v.finish([vb])
    lane8 = lane_iota(8)
    odd = c % 2 == 1

    def add1(i, carry):
        z2 = i + 4 * s + 2
        block, j = z2 // 4, z2 % 4
        for comp in range(3):
            at = (comp * (ns + 2) + block) * (y2 + 16) + (c // 2) * 8
            rows = wf[pl.ds(pl.multiple_of(at, 8), 24), :]
            value = jnp.where(odd, rows[10:18], rows[6:14])
            lane = lane8 % 4
            value = jnp.where(lane == j, value, 0.0)
            value = pair_sum(pair_sum(value, 1), 2)
            stage[pl.ds(0, 8, stride=2), :] = value
            stage[pl.ds(1, 8, stride=2), :] = value
            grown = stage[pl.ds(0, 16), :]
            for dz in range(2):
                p = g1.plane(comp, 2 * i + dz)
                inside = k1[g1.plane(0, 2 * i + dz), :] > 0.0
                va[p, :] = vb[p, :] + jnp.where(inside, grown, 0.0)
        return carry

    lax.fori_loop(0, g1.z // 2, add1, 0)
    level1.sweep(g1.oz - 3, g1.oz + n1 + 3, va, b1, vb)
    level1.sweep(g1.oz - 2, g1.oz + n1 + 2, vb, b1, va)

    ex_u.finish([ub, m0])

    def add0(z, carry):
        for comp in range(3):
            near = (z - g0.oz + 2 * g1.oz) // 2
            value = va[g1.plane(comp, near), :][2:14]
            stage[pl.ds(0, 12, stride=2), :] = value
            stage[pl.ds(1, 12, stride=2), :] = value
            p = g0.plane(comp, z)
            ua[p, :] = ub[p, :] + m0[g0.plane(0, z), :] * stage[pl.ds(0, g0.y), :]
        return carry

    lax.fori_loop(0, g0.z, add0, 0)
    level0.sweep(g0.oz - 2, g0.oz + n0 + 2, ua, b0, ub)
    level0.sweep(g0.oz - 1, g0.oz + n0 + 1, ub, b0, ua)

    def emit(comp, z, value):
        at = pl.ds(pl.multiple_of((comp * n0 + z - g0.oz) * y0, 8), y0)
        out_r[at, :] = value[g0.oy:g0.oy + y0]
        out_u[at, :] = ua[g0.plane(comp, z), :][g0.oy:g0.oy + y0]

    level0.residual(g0.oz, g0.oz + n0, ua, b0, m0, emit)

    def drain_one(t, carry):
        spread(t).wait_send()
        return carry

    lax.fori_loop(1, ns * nc, drain_one, 0)
    for ex_one in rounds:
        ex_one.drain()


def on_device(ns, nc, load, density, moduli, fixed):
    _, nz, ny, nx = load.shape
    g0 = Grid(nz, ny, 3, 4)
    g1 = Grid(nz // 2, ny // 2, 4, 4)
    ex = (
        (g0, ((1, 3), (1, 2), (3, 2))),
        (g1, ((1, 4),)),
        (g1, ((3, 3),)),
        (g0, ((3, 3), (1, 3))),
        (g1, ((3, 4),)),
    )
    buf = lambda rows: pltpu.VMEM((rows, LANES), F32)
    y2, y3 = 4 * nc, 2 * nc
    s2, s3 = (ns + 2) * y2, (ns + 2) * y3
    scratch = [buf(g0.rows)] * 2 + [buf(3 * g0.rows)] * 3 + [buf(g0.rows)] * 8
    scratch += [buf(g1.rows)] + [buf(3 * g1.rows)] * 3 + [buf(g1.rows)] * 8
    scratch += [buf(s2)] + [buf(3 * s2)] * 3 + [buf(3 * (ns + 2) * (y2 + 16))] + [buf(s2)] * 8
    scratch += [buf(s3)] + [buf(3 * s3)] * 3 + [buf(s3)] * 8
    scratch += [buf(16), buf(ns * nc * 16), buf(max(y2, 32))]
    for grid, fields in ex:
        sizes = [message(grid, dz, dy, fields)[1] for dz, dy in DIRS]
        scratch += [buf(n) for n in sizes] * 2
        scratch += [pltpu.SemaphoreType.DMA((8,))] * 2
    scratch += [pltpu.SemaphoreType.DMA((ns * nc,))] * 2

    def run(*args):
        kernel(ns, nc, g0, g1, ex, *args)

    rows = 3 * nz * ny
    vmem = pl.BlockSpec(memory_space=pltpu.VMEM)
    u, r = pl.pallas_call(
        run,
        out_shape=[jax.ShapeDtypeStruct((rows, nx), F32)] * 2,
        in_specs=[vmem, vmem, pl.BlockSpec(memory_space=pltpu.SMEM), vmem],
        out_specs=[vmem, vmem],
        scratch_shapes=scratch,
        compiler_params=pltpu.CompilerParams(has_side_effects=True, vmem_limit_bytes=56 * 1024 * 1024),
        name="vcycle",
    )(load.reshape(rows, nx), density.reshape(nz * ny, nx), moduli, fixed.reshape(nz * ny, nx))
    shape = (3, nz, ny, nx)
    return u.reshape(shape), r.reshape(shape)


def solution(mesh):
    ns, nc = mesh.shape["slab"], mesh.shape["col"]
    placed = (P(None, "slab", "col", None), P("slab", "col", None), P(), P("slab", "col", None))

    def body(load, density, moduli, fixed):
        return on_device(ns, nc, load, density, moduli, fixed)

    return jax.shard_map(
        body,
        mesh=mesh,
        in_specs=placed,
        out_specs=(P(None, "slab", "col", None), P(None, "slab", "col", None)),
        check_vma=False,
    )
```

time: 442 us -> 60.3 us (0.14)
  the two profiles are of different devices: /device:TPU:28 before, /device:TPU:0 now
where the time goes in v1:
time: 60.3 us; the launch traced here: 60.1 us
  Pallas kernels  56.9 us (94%)
  local copies, waits for them, and re-layouts  2.57 us (4%)
  between operations  0.65 us (1%)
    pallas_call x1, Pallas kernels, on_device(): pl.pallas_call(run, out_shape=[jax.ShapeDtypeStruct((rows, nx), F32)] * 2...  56.9 us
    unnamed x4, local copies, waits for them, and re-layouts  2.57 us

profile of v1, /device:TPU:0, one launch (start us, length us, event | category | flops | bytes accessed | tf_op | source)
XLA Modules:
  0.0 60.1 jit_solution(8130224123538004402)
XLA Ops:
  0.6 56.9 %vcycle.1 = (f32[768,128]{1,0:T(8,128)}, f32[768,128]{1,0:T(8,128)}) custom-call(f32[768,128]{1,0:T(8,128)} %bitcast.5, s32[256,128]{1,0:T(8,128)} %bitcast.8, f32[8]{0:T(128)} %args_2_.4, s32[256,128]{1,0:T(8,128)} %bitcast.9), custom_call_target="tpu_custom_call" | custom-call | tf_op jit(solution)/shard_map/vcycle/pallas_call | solution.py:543
  57.6 0.0 copy-start
  57.6 1.8 %copy.8 = f32[3,16,16,128]{3,2,1,0:T(8,128)} copy(f32[3,16,16,128]{3,2,1,0:T(8,128)} %bitcast.7) | data formatting | bytes 786432
  59.4 0.0 copy-done
  59.4 0.7 %copy.9 = f32[3,16,16,128]{3,2,1,0:T(8,128)} copy(f32[3,16,16,128]{3,2,1,0:T(8,128)S(1)} %bitcast.6) | data formatting | bytes 786432
Async XLA Ops:
  57.6 1.8 %copy-start = (f32[768,128]{1,0:T(8,128)S(1)}, f32[768,128]{1,0:T(8,128)}, u32[]{:S(2)}) copy-start(f32[768,128]{1,0:T(8,128)} %get-tuple-element.5) | copy-start | bytes 1179652

commit v2 on v1

--- a/solution.py
+++ b/solution.py
@@ -282,6 +282,15 @@
         rows = ref.shape[0]
         ref[...] = jnp.zeros((rows, LANES), F32)
 
+    barrier = pltpu.get_barrier_semaphore()
+
+    def greet(t, carry):
+        target = (lax.rem(s + t // nc, ns), lax.rem(c + t % nc, nc))
+        pl.semaphore_signal(barrier, inc=1, device_id=target, device_id_type=pl.DeviceIdType.MESH)
+        return carry
+
+    lax.fori_loop(1, ns * nc, greet, 0)
+
     for ref in (k0, m0, b0, k1):
         zero(ref)
 
@@ -302,6 +311,7 @@
         return carry
 
     lax.fori_loop(0, n0, fill, 0)
+    pl.semaphore_wait(barrier, ns * nc - 1)
     ex_a.start([k0, m0, b0])
 
     def coarser(src, grid, comp, z, y, count, steps):
@@ -358,7 +368,6 @@
         for z in range(n1):
             b1[pl.ds(g1.row(comp, z, 0), y1), :] = coarser(ua, g0, comp, z, 0, y1, (1,))
     ex_b.start([b1])
-    ex_u.start([ub, m0])
 
     ex_k.finish([k1])
     level1.setup(g1.oz - 3, g1.oz + n1 + 3, None)
@@ -379,7 +388,7 @@
     def spread(t):
         target = (lax.rem(s + t // nc, ns), lax.rem(c + t % nc, nc))
         return pltpu.make_async_remote_copy(
-            src_ref=gather.at[here], dst_ref=gather.at[here], send_sem=gsend.at[t], recv_sem=grecv.at[t],
+            src_ref=gather.at[here], dst_ref=gather.at[here], send_sem=gsend, recv_sem=grecv,
             device_id=target, device_id_type=pl.DeviceIdType.MESH)
 
     def start_one(t, carry):
@@ -387,13 +396,13 @@
         return carry
 
     lax.fori_loop(1, ns * nc, start_one, 0)
+    all_others = pl.ds(0, (ns * nc - 1) * 16)
+    everything = pltpu.make_async_remote_copy(
+        src_ref=gather.at[all_others], dst_ref=gather.at[all_others], send_sem=gsend, recv_sem=grecv,
+        device_id=(lax.rem(s + 1, ns), c), device_id_type=pl.DeviceIdType.MESH)
+    everything.wait_recv()
     ex_v.start([vb])
-
-    def wait_one(t, carry):
-        spread(t).wait_recv()
-        return carry
-
-    lax.fori_loop(1, ns * nc, wait_one, 0)
+    ex_u.start([ub, m0])
 
     def assemble(t, carry):
         z, pair = t // (nc // 2), t % (nc // 2)
@@ -501,11 +510,7 @@
 
     level0.residual(g0.oz, g0.oz + n0, ua, b0, m0, emit)
 
-    def drain_one(t, carry):
-        spread(t).wait_send()
-        return carry
-
-    lax.fori_loop(1, ns * nc, drain_one, 0)
+    everything.wait_send()
     for ex_one in rounds:
         ex_one.drain()
 
@@ -533,7 +538,7 @@
         sizes = [message(grid, dz, dy, fields)[1] for dz, dy in DIRS]
         scratch += [buf(n) for n in sizes] * 2
         scratch += [pltpu.SemaphoreType.DMA((8,))] * 2
-    scratch += [pltpu.SemaphoreType.DMA((ns * nc,))] * 2
+    scratch += [pltpu.SemaphoreType.DMA] * 2
 
     def run(*args):
         kernel(ns, nc, g0, g1, ex, *args)
@@ -546,7 +551,7 @@
         in_specs=[vmem, vmem, pl.BlockSpec(memory_space=pltpu.SMEM), vmem],
         out_specs=[vmem, vmem],
         scratch_shapes=scratch,
-        compiler_params=pltpu.CompilerParams(has_side_effects=True, vmem_limit_bytes=56 * 1024 * 1024),
+        compiler_params=pltpu.CompilerParams(collective_id=0, has_side_effects=True, vmem_limit_bytes=56 * 1024 * 1024),
         name="vcycle",
     )(load.reshape(rows, nx), density.reshape(nz * ny, nx), moduli, fixed.reshape(nz * ny, nx))
     shape = (3, nz, ny, nx)

time: 60.3 us -> 55.3 us (0.917)
  Pallas kernels: 56.9 us -> 51.9 us
    pallas_call x1, Pallas kernels: 56.9 us -> 51.9 us  [on_device(): pl.pallas_call(run, out_shape=[jax.ShapeDtypeStruct((rows, nx), F32)] * 2...]
where the time goes in v2:
time: 55.3 us; the launch traced here: 55.1 us
  Pallas kernels  51.9 us (94%)
  local copies, waits for them, and re-layouts  2.57 us (5%)
  between operations  0.65 us (1%)
    pallas_call x1, Pallas kernels, on_device(): pl.pallas_call(run, out_shape=[jax.ShapeDtypeStruct((rows, nx), F32)] * 2...  51.9 us
    unnamed x4, local copies, waits for them, and re-layouts  2.57 us

profile of v2, /device:TPU:0, one launch (start us, length us, event | category | flops | bytes accessed | tf_op | source)
XLA Modules:
  0.0 55.1 jit_solution(9016375045630422820)
XLA Ops:
  0.6 51.9 %vcycle.1 = (f32[768,128]{1,0:T(8,128)}, f32[768,128]{1,0:T(8,128)}) custom-call(f32[768,128]{1,0:T(8,128)} %bitcast.5, s32[256,128]{1,0:T(8,128)} %bitcast.8, f32[8]{0:T(128)} %args_2_.4, s32[256,128]{1,0:T(8,128)} %bitcast.9), custom_call_target="tpu_custom_call" | custom-call | tf_op jit(solution)/shard_map/vcycle/pallas_call | solution.py:548
  52.6 0.0 copy-start
  52.6 1.8 %copy.8 = f32[3,16,16,128]{3,2,1,0:T(8,128)} copy(f32[3,16,16,128]{3,2,1,0:T(8,128)} %bitcast.7) | data formatting | bytes 786432
  54.4 0.0 copy-done
  54.4 0.7 %copy.9 = f32[3,16,16,128]{3,2,1,0:T(8,128)} copy(f32[3,16,16,128]{3,2,1,0:T(8,128)S(1)} %bitcast.6) | data formatting | bytes 786432
Async XLA Ops:
  52.6 1.8 %copy-start = (f32[768,128]{1,0:T(8,128)S(1)}, f32[768,128]{1,0:T(8,128)}, u32[]{:S(2)}) copy-start(f32[768,128]{1,0:T(8,128)} %get-tuple-element.5) | copy-start | bytes 1179652

commit v3 on v2

--- a/solution.py
+++ b/solution.py
@@ -11,6 +11,7 @@
 COARSE_SWEEPS = 8
 LANES = 128
 F32 = jnp.float32
+LIVE = 27
 DIRS = ((0, 1), (0, -1), (1, 0), (-1, 0), (1, 1), (1, -1), (-1, 1), (-1, -1))
 
 
@@ -152,31 +153,55 @@
     return pl.ds(start, count)
 
 
+def loop(low, high, rows, plane, body):
+    count = high - low
+    unit = max(u for u in range(1, count + 1) if count % u == 0 and (u == 1 or 3 * u * rows <= 8 * LIVE))
+
+    def step(i, carry):
+        base = low + i * unit
+        held, todo = {}, []
+
+        def get(ref, comp, off):
+            key = (id(ref), comp, off)
+            if key not in held:
+                held[key] = ref[plane(comp, base + off), :]
+            return held[key]
+
+        for j in range(unit):
+            todo += body(lambda ref, comp, off, j=j: get(ref, comp, off + j), base + j)
+        for ref, at, value in todo:
+            ref[at, :] = value
+        return carry
+
+    if count == unit:
+        step(0, 0)
+    else:
+        lax.fori_loop(0, count // unit, step, 0)
+
+
 class Level:
-    def __init__(self, scale, xs, zs, group, ny, closed, plane, k, coef, size):
+    def __init__(self, scale, xs, zs, group, ny, closed, plane, k, coef):
         self.scale, self.xs, self.zs, self.group, self.ny, self.closed = scale, xs, zs, group, ny, closed
-        self.plane, self.k, self.coef, self.size = plane, k, coef, size
-
-    def at(self, which, z):
-        p = self.plane(0, z)
-        return self.coef[which][p, :]
-
-    def z_sides(self, get, z):
-        after, before = get(z + 1), get(z - 1)
+        self.plane, self.k, self.coef = plane, k, coef
+
+    def loop(self, low, high, body):
+        loop(low, high, self.ny, self.plane, body)
+
+    def z_sides(self, get):
+        after, before = get(1), get(-1)
         if not self.group:
             return after, before
-        here = get(z)
+        here = get(0)
         lane = lane_iota(self.ny) % self.group
         turn = self.group - self.zs
         return (jnp.where(lane < turn, left(here, self.zs), right(after, turn)),
                 jnp.where(lane >= self.zs, right(here, self.zs), left(before, turn)))
 
-    def setup(self, low, high, mask):
-        def body(z, carry):
-            get = lambda i: self.k[self.plane(0, i), :]
-            k = get(z)
+    def setup(self, low, high, mask, rhs, out):
+        def body(get, z):
+            k = get(self.k, 0, 0)
             lane = lane_iota(self.ny)
-            zp, zm = self.z_sides(get, z)
+            zp, zm = self.z_sides(lambda off: get(self.k, 0, off))
             inx = lane < LANES - self.xs
             inm = lane >= self.xs
             xp = jnp.where(inx, left(k, self.xs), 0.0)
@@ -197,62 +222,55 @@
             inside = k > 0.0
             diag = jnp.where(inside, total + F32(2.0 * COUPLE) * k, 1.0)
             weight = jnp.where(inside, F32(OMEGA) / diag, 0.0)
+            if mask is not None:
+                weight = weight * get(mask, 0, 0)
             p = self.plane(0, z)
-            if mask is not None:
-                weight = weight * mask[p, :]
-            for which, value in enumerate((kzp, kzm, kyp, kym, kxp, kxm, total + F32(COUPLE) * k, weight)):
-                self.coef[which][p, :] = value
-            return carry
-
-        lax.fori_loop(low, high, body, 0)
+            todo = [(self.coef[i], p, value) for i, value in
+                    enumerate((kzp, kzm, kyp, kym, kxp, kxm, total + F32(COUPLE) * k, weight))]
+            if rhs is not None:
+                todo += [(out, self.plane(c, z), weight * get(rhs, c, 0)) for c in range(3)]
+            return todo
+
+        self.loop(low, high, body)
 
     def first(self, low, high, rhs, out):
-        def body(z, carry):
-            weight = self.at(7, z)
-            for c in range(3):
-                p = self.plane(c, z)
-                out[p, :] = weight * rhs[p, :]
-            return carry
-
-        lax.fori_loop(low, high, body, 0)
-
-    def defect(self, z, u, rhs):
-        kzp, kzm, kyp, kym, kxp, kxm, own = [self.at(i, z) for i in range(7)]
-        couple = F32(COUPLE) * self.k[self.plane(0, z), :]
-        field = [u[self.plane(c, z), :] for c in range(3)]
+        self.loop(low, high, lambda get, z: [
+            (out, self.plane(c, z), get(self.coef[7], 0, 0) * get(rhs, c, 0)) for c in range(3)])
+
+    def defect(self, get, u, rhs):
+        kzp, kzm, kyp, kym, kxp, kxm, own = [get(self.coef[i], 0, 0) for i in range(7)]
+        couple = F32(COUPLE) * get(self.k, 0, 0)
+        field = [get(u, c, 0) for c in range(3)]
         shared = couple * (field[0] + field[1] + field[2])
         out = []
         for c in range(3):
             v = field[c]
-            zp, zm = self.z_sides(lambda i: u[self.plane(c, i), :], z)
+            zp, zm = self.z_sides(lambda off: get(u, c, off))
             near = (kzp * zp + kzm * zm) + (kyp * up(v) + kym * down(v))
             near = near + (kxp * left(v, self.xs) + kxm * right(v, self.xs))
-            out.append((rhs[self.plane(c, z), :] - shared) + (near - own * v))
+            out.append((get(rhs, c, 0) - shared) + (near - own * v))
         return field, out
 
     def sweep(self, low, high, u, rhs, out, out_plane=None):
         place = out_plane or self.plane
 
-        def body(z, carry):
-            field, out_d = self.defect(z, u, rhs)
-            weight = self.at(7, z)
+        def body(get, z):
+            field, delta = self.defect(get, u, rhs)
+            weight = get(self.coef[7], 0, 0)
+            return [(out, place(c, z), field[c] + weight * delta[c]) for c in range(3)]
+
+        self.loop(low, high, body)
+
+    def residual(self, low, high, u, rhs, mask, emit):
+        def body(get, z):
+            field, delta = self.defect(get, u, rhs)
+            todo = []
             for c in range(3):
-                out[place(c, z), :] = field[c] + weight * out_d[c]
-            return carry
-
-        lax.fori_loop(low, high, body, 0)
-
-    def residual(self, low, high, u, rhs, mask, out):
-        def body(z, carry):
-            _, out_d = self.defect(z, u, rhs)
-            for c in range(3):
-                value = out_d[c]
-                if mask is not None:
-                    value = mask[self.plane(0, z), :] * value
-                out(c, z, value)
-            return carry
-
-        lax.fori_loop(low, high, body, 0)
+                value = delta[c] if mask is None else get(mask, 0, 0) * delta[c]
+                todo += emit(c, z, value, field[c])
+            return todo
+
+        self.loop(low, high, body)
 
 
 def kernel(ns, nc, g0, g1, ex, load, dens, moduli, fixed, out_u, out_r, *scratch):
@@ -294,23 +312,19 @@
     for ref in (k0, m0, b0, k1):
         zero(ref)
 
-    def fill(z, carry):
-        src = pl.ds(pl.multiple_of(z * y0, 8), y0)
-        d = dens[src, :]
+    def fill(get, z):
+        d = get(dens, 0, 0)
         value = jnp.zeros((y0, LANES), F32)
         for klass in range(CLASSES):
             value = jnp.where(d == klass, moduli[klass], value)
-        keep = 1.0 - fixed[src, :].astype(F32)
+        keep = 1.0 - get(fixed, 0, 0).astype(F32)
         wide = lambda v: jnp.concatenate(
             [jnp.zeros((g0.oy, LANES), F32), v, jnp.zeros((g0.oy, LANES), F32)], axis=0)
-        k0[g0.plane(0, z + g0.oz), :] = wide(value)
-        m0[g0.plane(0, z + g0.oz), :] = wide(keep)
-        for comp in range(3):
-            at = pl.ds(pl.multiple_of((comp * n0 + z) * y0, 8), y0)
-            b0[g0.plane(comp, z + g0.oz), :] = wide(load[at, :])
-        return carry
-
-    lax.fori_loop(0, n0, fill, 0)
+        p = g0.plane(0, z + g0.oz)
+        return [(k0, p, wide(value)), (m0, p, wide(keep))] + [
+            (b0, g0.plane(comp, z + g0.oz), wide(get(load, comp, 0))) for comp in range(3)]
+
+    loop(0, n0, y0, lambda comp, z: rows_of((comp * n0 + z) * y0, y0), fill)
     pl.semaphore_wait(barrier, ns * nc - 1)
     ex_a.start([k0, m0, b0])
 
@@ -340,14 +354,14 @@
     for ref in (ua, ub, b1, va, vb):
         zero(ref)
 
-    level0 = Level(1.0, 1, 0, 0, g0.y, False, g0.plane, k0, c0, g0.z)
-    level1 = Level(0.25, 2, 0, 0, g1.y, False, g1.plane, k1, c1, g1.z)
+    level0 = Level(1.0, 1, 0, 0, g0.y, False, g0.plane, k0, c0)
+    level1 = Level(0.25, 2, 0, 0, g1.y, False, g1.plane, k1, c1)
     y2, y3 = 4 * nc, 2 * nc
     plane2 = lambda comp, z: rows_of((comp * (ns + 2) + z) * y2, y2)
     plane3 = lambda comp, z: rows_of((comp * (ns + 2) + z) * y3, y3)
     wide2 = lambda comp, z: rows_of((comp * (ns + 2) + z) * (y2 + 16) + 8, y2)
-    level2 = Level(0.25**2, 4, 1, 4, y2, True, plane2, k2, c2, ns)
-    level3 = Level(0.25**3, 8, 2, 4, y3, True, plane3, k3, c3, ns)
+    level2 = Level(0.25**2, 4, 1, 4, y2, True, plane2, k2, c2)
+    level3 = Level(0.25**3, 8, 2, 4, y3, True, plane3, k3, c3)
     for ref, comps, plane, rows in ((k2, 1, plane2, y2), (wa, 3, plane2, y2), (wb, 3, plane2, y2),
                                     (k3, 1, plane3, y3), (xa, 3, plane3, y3), (xb, 3, plane3, y3),
                                     (wf, 3, lambda comp, z: rows_of((comp * (ns + 2) + z) * (y2 + 16), y2 + 16), y2 + 16)):
@@ -356,12 +370,11 @@
                 ref[plane(comp, z), :] = jnp.zeros((rows, LANES), F32)
 
     ex_a.finish([k0, m0, b0])
-    level0.setup(g0.oz - 2, g0.oz + n0 + 2, m0)
-    level0.first(g0.oz - 2, g0.oz + n0 + 2, b0, ua)
+    level0.setup(g0.oz - 2, g0.oz + n0 + 2, m0, b0, ua)
     level0.sweep(g0.oz - 1, g0.oz + n0 + 1, ua, b0, ub)
 
-    def keep0(comp, z, value):
-        ua[g0.plane(comp, z), :] = value
+    def keep0(comp, z, value, field):
+        return [(ua, g0.plane(comp, z), value)]
 
     level0.residual(g0.oz, g0.oz + n0, ub, b0, m0, keep0)
     for comp in range(3):
@@ -370,13 +383,13 @@
     ex_b.start([b1])
 
     ex_k.finish([k1])
-    level1.setup(g1.oz - 3, g1.oz + n1 + 3, None)
+    level1.setup(g1.oz - 3, g1.oz + n1 + 3, None, None, None)
     ex_b.finish([b1])
     level1.first(g1.oz - 2, g1.oz + n1 + 2, b1, va)
     level1.sweep(g1.oz - 1, g1.oz + n1 + 1, va, b1, vb)
 
-    def keep1(comp, z, value):
-        va[g1.plane(comp, z), :] = value
+    def keep1(comp, z, value, field):
+        return [(va, g1.plane(comp, z), value)]
 
     level1.residual(g1.oz, g1.oz + n1, vb, b1, None, keep1)
     for comp in range(3):
@@ -415,12 +428,11 @@
         return carry
 
     lax.fori_loop(0, ns * nc // 2, assemble, 0)
-    level2.setup(1, ns + 1, None)
-    level2.first(1, ns + 1, b2, wa)
+    level2.setup(1, ns + 1, None, b2, wa)
     level2.sweep(1, ns + 1, wa, b2, wb)
 
-    def keep2(comp, z, value):
-        wa[plane2(comp, z), :] = value
+    def keep2(comp, z, value, field):
+        return [(wa, plane2(comp, z), value)]
 
     level2.residual(1, ns + 1, wb, b2, None, keep2)
 
@@ -432,31 +444,31 @@
         return carry
 
     lax.fori_loop(1, ns + 1, shrink3, 0)
-    level3.setup(1, ns + 1, None)
-    level3.first(1, ns + 1, b3, xa)
+    level3.setup(1, ns + 1, None, b3, xa)
     old, new = xa, xb
     for turn in range(COARSE_SWEEPS - 1):
         level3.sweep(1, ns + 1, old, b3, new)
         old, new = new, old
     coarse = old
 
+    def twice(value, slot):
+        rows = value.shape[0]
+        stage[pl.ds(slot, rows, stride=2), :] = value
+        stage[pl.ds(slot + 1, rows, stride=2), :] = value
+        return slot, 2 * rows
+
+    def staged(spot):
+        return stage[pl.ds(spot[0], spot[1]), :]
+
     def add2(z, carry):
+        spots = [twice(coarse[plane3(comp, z), :], comp * y2) for comp in range(3)]
         for comp in range(3):
-            value = coarse[plane3(comp, z), :]
-            stage[pl.ds(0, y3, stride=2), :] = value
-            stage[pl.ds(1, y3, stride=2), :] = value
             p = plane2(comp, z)
-            wb[p, :] = wb[p, :] + stage[pl.ds(0, y2), :]
+            wb[p, :] = wb[p, :] + staged(spots[comp])
         return carry
 
     lax.fori_loop(1, ns + 1, add2, 0)
 
-    def clear(ref):
-        for comp in range(3):
-            for z in (0, ns + 1):
-                ref[plane2(comp, z), :] = jnp.zeros((y2, LANES), F32)
-
-    clear(wa)
     level2.sweep(1, ns + 1, wb, b2, wa)
     level2.sweep(1, ns + 1, wa, b2, wf, wide2)
 
@@ -467,16 +479,15 @@
     def add1(i, carry):
         z2 = i + 4 * s + 2
         block, j = z2 // 4, z2 % 4
+        spots = []
         for comp in range(3):
             at = (comp * (ns + 2) + block) * (y2 + 16) + (c // 2) * 8
             rows = wf[pl.ds(pl.multiple_of(at, 8), 24), :]
             value = jnp.where(odd, rows[10:18], rows[6:14])
-            lane = lane8 % 4
-            value = jnp.where(lane == j, value, 0.0)
-            value = pair_sum(pair_sum(value, 1), 2)
-            stage[pl.ds(0, 8, stride=2), :] = value
-            stage[pl.ds(1, 8, stride=2), :] = value
-            grown = stage[pl.ds(0, 16), :]
+            value = jnp.where(lane8 % 4 == j, value, 0.0)
+            spots.append(twice(pair_sum(pair_sum(value, 1), 2), comp * 16))
+        for comp in range(3):
+            grown = staged(spots[comp])
             for dz in range(2):
                 p = g1.plane(comp, 2 * i + dz)
                 inside = k1[g1.plane(0, 2 * i + dz), :] > 0.0
@@ -489,24 +500,23 @@
 
     ex_u.finish([ub, m0])
 
-    def add0(z, carry):
+    def add0(i, carry):
+        spots = [twice(va[g1.plane(comp, i + g1.oz - 2), :][2:14], comp * g0.y) for comp in range(3)]
         for comp in range(3):
-            near = (z - g0.oz + 2 * g1.oz) // 2
-            value = va[g1.plane(comp, near), :][2:14]
-            stage[pl.ds(0, 12, stride=2), :] = value
-            stage[pl.ds(1, 12, stride=2), :] = value
-            p = g0.plane(comp, z)
-            ua[p, :] = ub[p, :] + m0[g0.plane(0, z), :] * stage[pl.ds(0, g0.y), :]
-        return carry
-
-    lax.fori_loop(0, g0.z, add0, 0)
+            grown = staged(spots[comp])
+            for dz in range(2):
+                p = g0.plane(comp, 2 * i + dz)
+                ua[p, :] = ub[p, :] + m0[g0.plane(0, 2 * i + dz), :] * grown
+        return carry
+
+    lax.fori_loop(0, g0.z // 2, add0, 0)
     level0.sweep(g0.oz - 2, g0.oz + n0 + 2, ua, b0, ub)
     level0.sweep(g0.oz - 1, g0.oz + n0 + 1, ub, b0, ua)
 
-    def emit(comp, z, value):
+    def emit(comp, z, value, field):
         at = pl.ds(pl.multiple_of((comp * n0 + z - g0.oz) * y0, 8), y0)
-        out_r[at, :] = value[g0.oy:g0.oy + y0]
-        out_u[at, :] = ua[g0.plane(comp, z), :][g0.oy:g0.oy + y0]
+        own = slice(g0.oy, g0.oy + y0)
+        return [(out_r, at, value[own]), (out_u, at, field[own])]
 
     level0.residual(g0.oz, g0.oz + n0, ua, b0, m0, emit)
 
@@ -517,7 +527,7 @@
 
 def on_device(ns, nc, load, density, moduli, fixed):
     _, nz, ny, nx = load.shape
-    g0 = Grid(nz, ny, 3, 4)
+    g0 = Grid(nz, ny, 4, 4)
     g1 = Grid(nz // 2, ny // 2, 4, 4)
     ex = (
         (g0, ((1, 3), (1, 2), (3, 2))),
@@ -533,12 +543,14 @@
     scratch += [buf(g1.rows)] + [buf(3 * g1.rows)] * 3 + [buf(g1.rows)] * 8
     scratch += [buf(s2)] + [buf(3 * s2)] * 3 + [buf(3 * (ns + 2) * (y2 + 16))] + [buf(s2)] * 8
     scratch += [buf(s3)] + [buf(3 * s3)] * 3 + [buf(s3)] * 8
-    scratch += [buf(16), buf(ns * nc * 16), buf(max(y2, 32))]
+    scratch += [buf(16), buf(ns * nc * 16), buf(3 * max(y2, g0.y))]
     for grid, fields in ex:
         sizes = [message(grid, dz, dy, fields)[1] for dz, dy in DIRS]
         scratch += [buf(n) for n in sizes] * 2
         scratch += [pltpu.SemaphoreType.DMA((8,))] * 2
     scratch += [pltpu.SemaphoreType.DMA] * 2
+
+    used = sum(4 * LANES * ref.shape[0] for ref in scratch if hasattr(ref, "shape"))
 
     def run(*args):
         kernel(ns, nc, g0, g1, ex, *args)
@@ -551,7 +563,7 @@
         in_specs=[vmem, vmem, pl.BlockSpec(memory_space=pltpu.SMEM), vmem],
         out_specs=[vmem, vmem],
         scratch_shapes=scratch,
-        compiler_params=pltpu.CompilerParams(collective_id=0, has_side_effects=True, vmem_limit_bytes=56 * 1024 * 1024),
+        compiler_params=pltpu.CompilerParams(collective_id=0, has_side_effects=True, vmem_limit_bytes=used + 8 * 1024 * 1024),
         name="vcycle",
     )(load.reshape(rows, nx), density.reshape(nz * ny, nx), moduli, fixed.reshape(nz * ny, nx))
     shape = (3, nz, ny, nx)

time: 55.3 us -> 48.5 us (0.88)
  the two profiles are of different devices: /device:TPU:0 before, /device:TPU:9 now
where the time goes in v3:
time: 48.5 us; the launch traced here: 48.3 us
  Pallas kernels  42.7 us (88%)
  local copies, waits for them, and re-layouts  4.94 us (10%)
  between operations  0.65 us (1%)
    pallas_call x1, Pallas kernels, on_device(): pl.pallas_call(run, out_shape=[jax.ShapeDtypeStruct((rows, nx), F32)] * 2...  42.7 us
    unnamed x10, local copies, waits for them, and re-layouts  4.94 us

profile of v3, /device:TPU:9, one launch (start us, length us, event | category | flops | bytes accessed | tf_op | source)
XLA Modules:
  0.0 48.3 jit_solution(2422470174882960935)
XLA Ops:
  0.6 0.0 copy-start.3
  0.6 0.6 %copy-done.3 = f32[8]{0:T(128)S(1)} copy-done((f32[8]{0:T(128)S(1)}, f32[8]{0:T(128)}, u32[]{:S(2)}) %copy-start.3) | copy-done | bytes 56
  1.3 0.0 copy-start
  1.3 1.0 %copy-done = f32[3,16,16,128]{3,2,1,0:T(8,128)S(1)} copy-done((f32[3,16,16,128]{3,2,1,0:T(8,128)S(1)}, f32[3,16,16,128]{3,2,1,0:T(8,128)}, u32[]{:S(2)}) %copy-start) | copy-done | bytes 393240
  2.3 0.0 copy-start.1
  2.3 0.9 %copy-done.1 = s32[16,16,128]{2,1,0:T(8,128)S(1)} copy-done((s32[16,16,128]{2,1,0:T(8,128)S(1)}, s32[16,16,128]{2,1,0:T(8,128)}, u32[]{:S(2)}) %copy-start.1) | copy-done | bytes 131096
  3.2 0.0 copy-start.2
  3.2 0.9 %copy-done.2 = s32[16,16,128]{2,1,0:T(8,128)S(1)} copy-done((s32[16,16,128]{2,1,0:T(8,128)S(1)}, s32[16,16,128]{2,1,0:T(8,128)}, u32[]{:S(2)}) %copy-start.2) | copy-done | bytes 131096
  4.1 42.7 %vcycle.1 = (f32[768,128]{1,0:T(8,128)S(1)}, f32[768,128]{1,0:T(8,128)S(1)}) custom-call(f32[768,128]{1,0:T(8,128)S(1)} %bitcast.5, s32[256,128]{1,0:T(8,128)S(1)} %bitcast.8, f32[8]{0:T(128)S(1)} %copy-done.3, s32[256,128]{1,0:T(8,128)S(1)} %bitcast.9), custom_call_target="tpu_custom_call" | custom-call | tf_op jit(solution)/shard_map/vcycle/pallas_call | solution.py:560
  46.8 0.7 %copy.8 = f32[3,16,16,128]{3,2,1,0:T(8,128)} copy(f32[3,16,16,128]{3,2,1,0:T(8,128)S(1)} %bitcast.7) | data formatting | bytes 786432
  47.5 0.7 %copy.9 = f32[3,16,16,128]{3,2,1,0:T(8,128)} copy(f32[3,16,16,128]{3,2,1,0:T(8,128)S(1)} %bitcast.6) | data formatting | bytes 786432
Async XLA Ops:
  0.6 0.7 %copy-start.3 = (f32[8]{0:T(128)S(1)}, f32[8]{0:T(128)}, u32[]{:S(2)}) copy-start(f32[8]{0:T(128)} %args_2_.4) | copy-start | bytes 100
  1.3 1.0 %copy-start = (f32[3,16,16,128]{3,2,1,0:T(8,128)S(1)}, f32[3,16,16,128]{3,2,1,0:T(8,128)}, u32[]{:S(2)}) copy-start(f32[3,16,16,128]{3,2,1,0:T(8,128)} %param.4) | copy-start | bytes 1179652
  2.3 0.9 %copy-start.1 = (s32[16,16,128]{2,1,0:T(8,128)S(1)}, s32[16,16,128]{2,1,0:T(8,128)}, u32[]{:S(2)}) copy-start(s32[16,16,128]{2,1,0:T(8,128)} %param.5) | copy-start | bytes 393220
  3.2 0.9 %copy-start.2 = (s32[16,16,128]{2,1,0:T(8,128)S(1)}, s32[16,16,128]{2,1,0:T(8,128)}, u32[]{:S(2)}) copy-start(s32[16,16,128]{2,1,0:T(8,128)} %param.7) | copy-start | bytes 393220

commit v4 on v3

--- a/solution.py
+++ b/solution.py
@@ -72,6 +72,31 @@
     return pl.ds(start, count)
 
 
+def beside(here, step, count):
+    if not isinstance(step, int):
+        return lax.rem(here + step, count)
+    if step == 0:
+        return here
+    if step > 0:
+        return jnp.where(here >= count - step, here + (step - count), here + step)
+    return jnp.where(here < -step, here + (step + count), here + step)
+
+
+def others(ns, nc, body):
+    if ns * nc <= 32:
+        for a in range(ns):
+            for b in range(nc):
+                if a or b:
+                    body(a, b)
+        return
+
+    def one(t, carry):
+        body(t // nc, t % nc)
+        return carry
+
+    lax.fori_loop(1, ns * nc, one, 0)
+
+
 class Exchange:
     def __init__(self, grid, fields, where, send, recv, ssem, rsem):
         self.grid, self.fields, self.where = grid, fields, where
@@ -80,7 +105,7 @@
     def copy(self, d):
         dz, dy = DIRS[d]
         s, c, ns, nc = self.where
-        target = (lax.rem(s + dz + ns, ns), lax.rem(c + dy + nc, nc))
+        target = (beside(s, dz, ns), beside(c, dy, nc))
         return pltpu.make_async_remote_copy(
             src_ref=self.send[d], dst_ref=self.recv[d], send_sem=self.ssem.at[d], recv_sem=self.rsem.at[d],
             device_id=target, device_id_type=pl.DeviceIdType.MESH)
@@ -273,7 +298,7 @@
         self.loop(low, high, body)
 
 
-def kernel(ns, nc, g0, g1, ex, load, dens, moduli, fixed, out_u, out_r, *scratch):
+def kernel(ns, nc, g0, g1, ex, load_in, dens_in, moduli_in, fixed_in, out_u, out_r, *scratch):
     it = iter(scratch)
     take = lambda n: [next(it) for _ in range(n)]
     k0, m0, b0, ua, ub = take(5)
@@ -294,6 +319,11 @@
         rounds.append(Exchange(grid, fields, where, send, recv, ssem, rsem))
     gsend, grecv = take(2)
     ex_a, ex_k, ex_b, ex_u, ex_v = rounds
+    load, dens, moduli, fixed, arrived = take(5)
+    fetches = [pltpu.make_async_copy(src, dst, arrived.at[i]) for i, (src, dst) in enumerate(
+        ((dens_in, dens), (moduli_in, moduli), (fixed_in, fixed), (load_in, load)))]
+    for fetch in fetches:
+        fetch.start()
     n0, y0, n1, y1 = g0.nz, g0.ny, g1.nz, g1.ny
 
     def zero(ref):
@@ -302,12 +332,11 @@
 
     barrier = pltpu.get_barrier_semaphore()
 
-    def greet(t, carry):
-        target = (lax.rem(s + t // nc, ns), lax.rem(c + t % nc, nc))
+    def greet(a, b):
+        target = (beside(s, a, ns), beside(c, b, nc))
         pl.semaphore_signal(barrier, inc=1, device_id=target, device_id_type=pl.DeviceIdType.MESH)
-        return carry
-
-    lax.fori_loop(1, ns * nc, greet, 0)
+
+    others(ns, nc, greet)
 
     for ref in (k0, m0, b0, k1):
         zero(ref)
@@ -324,6 +353,8 @@
         return [(k0, p, wide(value)), (m0, p, wide(keep))] + [
             (b0, g0.plane(comp, z + g0.oz), wide(get(load, comp, 0))) for comp in range(3)]
 
+    for fetch in fetches:
+        fetch.wait()
     loop(0, n0, y0, lambda comp, z: rows_of((comp * n0 + z) * y0, y0), fill)
     pl.semaphore_wait(barrier, ns * nc - 1)
     ex_a.start([k0, m0, b0])
@@ -398,36 +429,36 @@
     here = pl.ds(pl.multiple_of((s * nc + c) * 16, 16), 16)
     gather[here, :] = pack[...]
 
-    def spread(t):
-        target = (lax.rem(s + t // nc, ns), lax.rem(c + t % nc, nc))
-        return pltpu.make_async_remote_copy(
+    def spread(a, b):
+        target = (beside(s, a, ns), beside(c, b, nc))
+        pltpu.make_async_remote_copy(
             src_ref=gather.at[here], dst_ref=gather.at[here], send_sem=gsend, recv_sem=grecv,
-            device_id=target, device_id_type=pl.DeviceIdType.MESH)
-
-    def start_one(t, carry):
-        spread(t).start()
-        return carry
-
-    lax.fori_loop(1, ns * nc, start_one, 0)
+            device_id=target, device_id_type=pl.DeviceIdType.MESH).start()
+
+    others(ns, nc, spread)
     all_others = pl.ds(0, (ns * nc - 1) * 16)
     everything = pltpu.make_async_remote_copy(
         src_ref=gather.at[all_others], dst_ref=gather.at[all_others], send_sem=gsend, recv_sem=grecv,
-        device_id=(lax.rem(s + 1, ns), c), device_id_type=pl.DeviceIdType.MESH)
+        device_id=(beside(s, 1, ns), c), device_id_type=pl.DeviceIdType.MESH)
     everything.wait_recv()
     ex_v.start([vb])
     ex_u.start([ub, m0])
 
     def assemble(t, carry):
         z, pair = t // (nc // 2), t % (nc // 2)
-        first = gather[pl.ds(pl.multiple_of(t * 32, 32), 16), :]
-        second = gather[pl.ds(pl.multiple_of(t * 32 + 16, 16), 16), :]
+        first = gather[rows_of(t * 32, 16), :]
+        second = gather[rows_of(t * 32 + 16, 16), :]
         for f in range(4):
             value = jnp.concatenate([first[4 * f:4 * f + 4], second[4 * f:4 * f + 4]], axis=0)
             ref, comp = (k2, 0) if f == 3 else (b2, f)
-            ref[pl.ds(pl.multiple_of((comp * (ns + 2) + z + 1) * y2 + pair * 8, 8), 8), :] = value
+            ref[rows_of((comp * (ns + 2) + z + 1) * y2 + pair * 8, 8), :] = value
         return carry
 
-    lax.fori_loop(0, ns * nc // 2, assemble, 0)
+    if ns * nc <= 32:
+        for t in range(ns * nc // 2):
+            assemble(t, 0)
+    else:
+        lax.fori_loop(0, ns * nc // 2, assemble, 0)
     level2.setup(1, ns + 1, None, b2, wa)
     level2.sweep(1, ns + 1, wa, b2, wb)
 
@@ -476,25 +507,21 @@
     lane8 = lane_iota(8)
     odd = c % 2 == 1
 
-    def add1(i, carry):
-        z2 = i + 4 * s + 2
-        block, j = z2 // 4, z2 % 4
+    for i in range(g1.z // 2):
+        block, j = s + (i + 2) // 4, (i + 2) % 4
         spots = []
         for comp in range(3):
             at = (comp * (ns + 2) + block) * (y2 + 16) + (c // 2) * 8
             rows = wf[pl.ds(pl.multiple_of(at, 8), 24), :]
             value = jnp.where(odd, rows[10:18], rows[6:14])
             value = jnp.where(lane8 % 4 == j, value, 0.0)
-            spots.append(twice(pair_sum(pair_sum(value, 1), 2), comp * 16))
+            spots.append(twice(pair_sum(pair_sum(value, 1), 2), (i % 2 * 3 + comp) * 16))
         for comp in range(3):
             grown = staged(spots[comp])
             for dz in range(2):
                 p = g1.plane(comp, 2 * i + dz)
                 inside = k1[g1.plane(0, 2 * i + dz), :] > 0.0
                 va[p, :] = vb[p, :] + jnp.where(inside, grown, 0.0)
-        return carry
-
-    lax.fori_loop(0, g1.z // 2, add1, 0)
     level1.sweep(g1.oz - 3, g1.oz + n1 + 3, va, b1, vb)
     level1.sweep(g1.oz - 2, g1.oz + n1 + 2, vb, b1, va)
 
@@ -543,24 +570,25 @@
     scratch += [buf(g1.rows)] + [buf(3 * g1.rows)] * 3 + [buf(g1.rows)] * 8
     scratch += [buf(s2)] + [buf(3 * s2)] * 3 + [buf(3 * (ns + 2) * (y2 + 16))] + [buf(s2)] * 8
     scratch += [buf(s3)] + [buf(3 * s3)] * 3 + [buf(s3)] * 8
-    scratch += [buf(16), buf(ns * nc * 16), buf(3 * max(y2, g0.y))]
+    scratch += [buf(16), buf(ns * nc * 16), buf(3 * max(y2, 32))]
     for grid, fields in ex:
         sizes = [message(grid, dz, dy, fields)[1] for dz, dy in DIRS]
         scratch += [buf(n) for n in sizes] * 2
         scratch += [pltpu.SemaphoreType.DMA((8,))] * 2
     scratch += [pltpu.SemaphoreType.DMA] * 2
 
-    used = sum(4 * LANES * ref.shape[0] for ref in scratch if hasattr(ref, "shape"))
-
     def run(*args):
         kernel(ns, nc, g0, g1, ex, *args)
 
     rows = 3 * nz * ny
+    scratch += [buf(rows), pltpu.VMEM((nz * ny, LANES), jnp.int32), pltpu.SMEM((CLASSES,), F32),
+                pltpu.VMEM((nz * ny, LANES), jnp.int32), pltpu.SemaphoreType.DMA((4,))]
+    used = sum(4 * LANES * ref.shape[0] for ref in scratch if hasattr(ref, "shape"))
     vmem = pl.BlockSpec(memory_space=pltpu.VMEM)
     u, r = pl.pallas_call(
         run,
         out_shape=[jax.ShapeDtypeStruct((rows, nx), F32)] * 2,
-        in_specs=[vmem, vmem, pl.BlockSpec(memory_space=pltpu.SMEM), vmem],
+        in_specs=[pl.BlockSpec(memory_space=pltpu.HBM)] * 4,
         out_specs=[vmem, vmem],
         scratch_shapes=scratch,
         compiler_params=pltpu.CompilerParams(collective_id=0, has_side_effects=True, vmem_limit_bytes=used + 8 * 1024 * 1024),

time: 48.5 us -> 47.5 us (0.979)
  Pallas kernels: 42.7 us -> 41.7 us
    pallas_call x1, Pallas kernels: 42.7 us -> 41.7 us  [on_device(): pl.pallas_call(run, out_shape=[jax.ShapeDtypeStruct((rows, nx), F32)] * 2...]
where the time goes in v4:
time: 47.5 us; the launch traced here: 47.3 us
  Pallas kernels  41.7 us (88%)
  local copies, waits for them, and re-layouts  4.94 us (10%)
  between operations  0.65 us (1%)
    pallas_call x1, Pallas kernels, on_device(): pl.pallas_call(run, out_shape=[jax.ShapeDtypeStruct((rows, nx), F32)] * 2...  41.7 us
    unnamed x10, local copies, waits for them, and re-layouts  4.94 us

profile of v4, /device:TPU:9, one launch (start us, length us, event | category | flops | bytes accessed | tf_op | source)
XLA Modules:
  0.0 47.3 jit_solution(7505646831376447702)
XLA Ops:
  0.6 0.0 copy-start.3
  0.6 0.6 %copy-done.3 = f32[8]{0:T(128)S(1)} copy-done((f32[8]{0:T(128)S(1)}, f32[8]{0:T(128)}, u32[]{:S(2)}) %copy-start.3) | copy-done | bytes 56
  1.3 0.0 copy-start
  1.3 1.0 %copy-done = f32[3,16,16,128]{3,2,1,0:T(8,128)S(1)} copy-done((f32[3,16,16,128]{3,2,1,0:T(8,128)S(1)}, f32[3,16,16,128]{3,2,1,0:T(8,128)}, u32[]{:S(2)}) %copy-start) | copy-done | bytes 393240
  2.3 0.0 copy-start.1
  2.3 0.9 %copy-done.1 = s32[16,16,128]{2,1,0:T(8,128)S(1)} copy-done((s32[16,16,128]{2,1,0:T(8,128)S(1)}, s32[16,16,128]{2,1,0:T(8,128)}, u32[]{:S(2)}) %copy-start.1) | copy-done | bytes 131096
  3.2 0.0 copy-start.2
  3.2 0.9 %copy-done.2 = s32[16,16,128]{2,1,0:T(8,128)S(1)} copy-done((s32[16,16,128]{2,1,0:T(8,128)S(1)}, s32[16,16,128]{2,1,0:T(8,128)}, u32[]{:S(2)}) %copy-start.2) | copy-done | bytes 131096
  4.1 41.7 %vcycle.1 = (f32[768,128]{1,0:T(8,128)S(1)}, f32[768,128]{1,0:T(8,128)S(1)}) custom-call(f32[768,128]{1,0:T(8,128)S(1)} %bitcast.5, s32[256,128]{1,0:T(8,128)S(1)} %bitcast.8, f32[8]{0:T(128)S(1)} %copy-done.3, s32[256,128]{1,0:T(8,128)S(1)} %bitcast.9), custom_call_target="tpu_custom_call" | custom-call | tf_op jit(solution)/shard_map/vcycle/pallas_call | solution.py:588
  45.8 0.7 %copy.8 = f32[3,16,16,128]{3,2,1,0:T(8,128)} copy(f32[3,16,16,128]{3,2,1,0:T(8,128)S(1)} %bitcast.7) | data formatting | bytes 786432
  46.6 0.7 %copy.9 = f32[3,16,16,128]{3,2,1,0:T(8,128)} copy(f32[3,16,16,128]{3,2,1,0:T(8,128)S(1)} %bitcast.6) | data formatting | bytes 786432
Async XLA Ops:
  0.6 0.7 %copy-start.3 = (f32[8]{0:T(128)S(1)}, f32[8]{0:T(128)}, u32[]{:S(2)}) copy-start(f32[8]{0:T(128)} %args_2_.4) | copy-start | bytes 100
  1.3 1.0 %copy-start = (f32[3,16,16,128]{3,2,1,0:T(8,128)S(1)}, f32[3,16,16,128]{3,2,1,0:T(8,128)}, u32[]{:S(2)}) copy-start(f32[3,16,16,128]{3,2,1,0:T(8,128)} %param.4) | copy-start | bytes 1179652
  2.3 0.9 %copy-start.1 = (s32[16,16,128]{2,1,0:T(8,128)S(1)}, s32[16,16,128]{2,1,0:T(8,128)}, u32[]{:S(2)}) copy-start(s32[16,16,128]{2,1,0:T(8,128)} %param.5) | copy-start | bytes 393220
  3.2 0.9 %copy-start.2 = (s32[16,16,128]{2,1,0:T(8,128)S(1)}, s32[16,16,128]{2,1,0:T(8,128)}, u32[]{:S(2)}) copy-start(s32[16,16,128]{2,1,0:T(8,128)} %param.7) | copy-start | bytes 393220

commit v5 on v4

--- a/solution.py
+++ b/solution.py
@@ -1,3 +1,5 @@
+import math
+
 import jax
 import jax.numpy as jnp
 from jax import lax
@@ -31,7 +33,7 @@
         return pl.ds(start, self.y)
 
 
-def segments(grid, dz, dy, depth):
+def segments(grid, dz, dy, low, depth):
     nz, ny = grid.nz, grid.ny
 
     def cell(step, d, n):
@@ -39,29 +41,31 @@
 
     out = []
     if dz == 0:
-        for i in range(1, depth + 1):
+        for i in range(low, depth + 1):
             mine, there = cell(i, dy, ny)
             out.append((0, mine, 0, there, nz, True))
     elif dy == 0:
-        for i in range(1, depth + 1):
+        for i in range(low, depth + 1):
             mine, there = cell(i, dz, nz)
             out.append((mine, 0, there, 0, ny, False))
     else:
         for i in range(1, depth):
-            for j in range(1, depth + 1 - i):
+            for j in range(max(1, low - i), depth + 1 - i):
                 mz, tz = cell(i, dz, nz)
                 my, ty = cell(j, dy, ny)
                 out.append((mz, my, tz, ty, 1, False))
     return out
 
 
-def message(grid, dz, dy, fields):
+def message(grid, dz, dy, fields, pairs):
+    runs = [(field, comp, seg) for field, (comps, low, depth) in enumerate(fields) for comp in range(comps)
+            for seg in segments(grid, dz, dy, low, depth)]
+    width = 2 if pairs else 1
     out, at = [], 0
-    for field, (comps, depth) in enumerate(fields):
-        for comp in range(comps):
-            for seg in segments(grid, dz, dy, depth):
-                out.append((field, comp, seg, at))
-                at += seg[4]
+    for first in range(0, len(runs), width):
+        part = runs[first:first + width]
+        out.append((part, at))
+        at += part[0][2][4]
     return out, -(-at // 8) * 8
 
 
@@ -98,8 +102,8 @@
 
 
 class Exchange:
-    def __init__(self, grid, fields, where, send, recv, ssem, rsem):
-        self.grid, self.fields, self.where = grid, fields, where
+    def __init__(self, grid, fields, pairs, where, send, recv, ssem, rsem):
+        self.grid, self.fields, self.pairs, self.where = grid, fields, pairs, where
         self.send, self.recv, self.ssem, self.rsem = send, recv, ssem, rsem
 
     def copy(self, d):
@@ -121,23 +125,34 @@
 
     def start(self, refs):
         for d, (dz, dy) in enumerate(DIRS):
-            rows, _ = message(self.grid, dz, dy, self.fields)
+            parts, _ = message(self.grid, dz, dy, self.fields, self.pairs)
 
             @pl.when(self.exists(dz, dy))
             def _():
-                for field, comp, (z, y, _, _, count, along), at in rows:
-                    self.send[d][pl.ds(at, count), :] = refs[field][window(self.grid, comp, z, y, count, along), :]
+                for runs, at in parts:
+                    values = [refs[field][window(self.grid, comp, z, y, count, along), :]
+                              for field, comp, (z, y, _, _, count, along) in runs]
+                    value = values[0]
+                    if len(values) == 2:
+                        value = jnp.where(lane_iota(value.shape[0]) % 2 == 0, value, values[1])
+                    self.send[d][pl.ds(at, value.shape[0]), :] = value
                 self.copy(d).start()
 
     def finish(self, refs):
         for d, (dz, dy) in enumerate(DIRS):
-            rows, _ = message(self.grid, dz, dy, self.fields)
+            parts, _ = message(self.grid, dz, dy, self.fields, self.pairs)
 
             @pl.when(self.exists(-dz, -dy))
             def _():
                 self.copy(d).wait_recv()
-                for field, comp, (_, _, z, y, count, along), at in rows:
-                    refs[field][window(self.grid, comp, z, y, count, along), :] = self.recv[d][pl.ds(at, count), :]
+                for runs, at in parts:
+                    value = self.recv[d][pl.ds(at, runs[0][2][4]), :]
+                    values = [value]
+                    if len(runs) == 2:
+                        even = lane_iota(value.shape[0]) % 2 == 0
+                        values = [jnp.where(even, value, right(value, 1)), jnp.where(even, left(value, 1), value)]
+                    for (field, comp, (_, _, z, y, count, along)), value in zip(runs, values):
+                        refs[field][window(self.grid, comp, z, y, count, along), :] = value
 
     def drain(self):
         for d, (dz, dy) in enumerate(DIRS):
@@ -222,7 +237,7 @@
         return (jnp.where(lane < turn, left(here, self.zs), right(after, turn)),
                 jnp.where(lane >= self.zs, right(here, self.zs), left(before, turn)))
 
-    def setup(self, low, high, mask, rhs, out):
+    def setup(self, low, high):
         def body(get, z):
             k = get(self.k, 0, 0)
             lane = lane_iota(self.ny)
@@ -247,20 +262,21 @@
             inside = k > 0.0
             diag = jnp.where(inside, total + F32(2.0 * COUPLE) * k, 1.0)
             weight = jnp.where(inside, F32(OMEGA) / diag, 0.0)
+            p = self.plane(0, z)
+            return [(self.coef[i], p, value) for i, value in
+                    enumerate((kzp, kzm, kyp, kym, kxp, kxm, total + F32(COUPLE) * k, weight))]
+
+        self.loop(low, high, body)
+
+    def first(self, low, high, rhs, out, mask=None):
+        def body(get, z):
+            weight, todo = get(self.coef[7], 0, 0), []
             if mask is not None:
                 weight = weight * get(mask, 0, 0)
-            p = self.plane(0, z)
-            todo = [(self.coef[i], p, value) for i, value in
-                    enumerate((kzp, kzm, kyp, kym, kxp, kxm, total + F32(COUPLE) * k, weight))]
-            if rhs is not None:
-                todo += [(out, self.plane(c, z), weight * get(rhs, c, 0)) for c in range(3)]
-            return todo
+                todo = [(self.coef[7], self.plane(0, z), weight)]
+            return todo + [(out, self.plane(c, z), weight * get(rhs, c, 0)) for c in range(3)]
 
         self.loop(low, high, body)
-
-    def first(self, low, high, rhs, out):
-        self.loop(low, high, lambda get, z: [
-            (out, self.plane(c, z), get(self.coef[7], 0, 0) * get(rhs, c, 0)) for c in range(3)])
 
     def defect(self, get, u, rhs):
         kzp, kzm, kyp, kym, kxp, kxm, own = [get(self.coef[i], 0, 0) for i in range(7)]
@@ -309,16 +325,15 @@
     c2 = take(8)
     k3, b3, xa, xb = take(4)
     c3 = take(8)
-    pack, gather, stage = take(3)
+    gk, gb, stage = take(3)
     s, c = lax.axis_index("slab"), lax.axis_index("col")
     where = (s, c, ns, nc)
     rounds = []
-    for grid, fields in ex:
+    for grid, fields, pairs in ex:
         send, recv = take(8), take(8)
         ssem, rsem = take(2)
-        rounds.append(Exchange(grid, fields, where, send, recv, ssem, rsem))
-    gsend, grecv = take(2)
-    ex_a, ex_k, ex_b, ex_u, ex_v = rounds
+        rounds.append(Exchange(grid, fields, pairs, where, send, recv, ssem, rsem))
+    ex_s, ex_a, ex_k, ex_b, ex_u, ex_v = rounds
     load, dens, moduli, fixed, arrived = take(5)
     fetches = [pltpu.make_async_copy(src, dst, arrived.at[i]) for i, (src, dst) in enumerate(
         ((dens_in, dens), (moduli_in, moduli), (fixed_in, fixed), (load_in, load)))]
@@ -357,7 +372,8 @@
         fetch.wait()
     loop(0, n0, y0, lambda comp, z: rows_of((comp * n0 + z) * y0, y0), fill)
     pl.semaphore_wait(barrier, ns * nc - 1)
-    ex_a.start([k0, m0, b0])
+    ex_s.start([k0])
+    ex_a.start([m0, b0])
 
     def coarser(src, grid, comp, z, y, count, steps):
         total = None
@@ -375,13 +391,44 @@
 
     lane4 = lane_iota(4) % 4
 
-    def packed(src, comp, slot):
+    here = s * nc + c
+
+    def packed(src, comp):
         value = jnp.zeros((4, LANES), F32)
         for z in range(n1 // 2):
             value = jnp.where(lane4 == z, coarser(src, g1, comp, z, 0, y1 // 2, (2,)), value)
-        pack[pl.ds(4 * slot, 4), :] = value
-
-    packed(k1, 0, 3)
+        return value
+
+    def gather(ref, comps, send_sem, recv_sem):
+        own = pl.ds(here * comps, comps)
+
+        def spread(a, b):
+            pltpu.make_async_remote_copy(
+                src_ref=ref.at[own], dst_ref=ref.at[own], send_sem=send_sem, recv_sem=recv_sem,
+                device_id=(beside(s, a, ns), beside(c, b, nc)), device_id_type=pl.DeviceIdType.MESH).start()
+
+        others(ns, nc, spread)
+        rest = pl.ds(0, (ns * nc - 1) * comps)
+        return pltpu.make_async_remote_copy(
+            src_ref=ref.at[rest], dst_ref=ref.at[rest], send_sem=send_sem, recv_sem=recv_sem,
+            device_id=(beside(s, 1, ns), c), device_id_type=pl.DeviceIdType.MESH)
+
+    def assemble(ref, comps, out):
+        def one(t, carry):
+            z, pair = t // (nc // 2), t % (nc // 2)
+            for comp in range(comps):
+                value = jnp.concatenate([ref[2 * t * comps + comp], ref[(2 * t + 1) * comps + comp]], axis=0)
+                out[rows_of((comp * (ns + 2) + z + 1) * y2 + pair * 8, 8), :] = value
+            return carry
+
+        if ns * nc <= 32:
+            for t in range(ns * nc // 2):
+                one(t, 0)
+        else:
+            lax.fori_loop(0, ns * nc // 2, one, 0)
+
+    gk[here] = packed(k1, 0)
+    all_k = gather(gk, 1, *take(2))
     for ref in (ua, ub, b1, va, vb):
         zero(ref)
 
@@ -400,8 +447,10 @@
             for z in (0, ns + 1):
                 ref[plane(comp, z), :] = jnp.zeros((rows, LANES), F32)
 
-    ex_a.finish([k0, m0, b0])
-    level0.setup(g0.oz - 2, g0.oz + n0 + 2, m0, b0, ua)
+    ex_s.finish([k0])
+    level0.setup(g0.oz - 2, g0.oz + n0 + 2)
+    ex_a.finish([m0, b0])
+    level0.first(g0.oz - 2, g0.oz + n0 + 2, b0, ua, m0)
     level0.sweep(g0.oz - 1, g0.oz + n0 + 1, ua, b0, ub)
 
     def keep0(comp, z, value, field):
@@ -414,8 +463,29 @@
     ex_b.start([b1])
 
     ex_k.finish([k1])
-    level1.setup(g1.oz - 3, g1.oz + n1 + 3, None, None, None)
+    level1.setup(g1.oz - 3, g1.oz + n1 + 3)
+    all_k.wait_recv()
+    assemble(gk, 1, k2)
+    level2.setup(1, ns + 1)
+
+    def shrink3(pairs):
+        def body(z, carry):
+            for src, dst, comp in pairs:
+                start = (comp * (ns + 2) + z) * y2
+                total = src[pl.ds(start, y3, stride=2), :] + src[pl.ds(start + 1, y3, stride=2), :]
+                dst[plane3(comp, z), :] = pair_sum(pair_sum(total, 1), 4) * F32(0.125)
+            return carry
+
+        if ns <= 4:
+            for z in range(1, ns + 1):
+                body(z, 0)
+        else:
+            lax.fori_loop(1, ns + 1, body, 0)
+
+    shrink3([(k2, k3, 0)])
+    level3.setup(1, ns + 1)
     ex_b.finish([b1])
+    ex_u.start([ub, m0])
     level1.first(g1.oz - 2, g1.oz + n1 + 2, b1, va)
     level1.sweep(g1.oz - 1, g1.oz + n1 + 1, va, b1, vb)
 
@@ -424,42 +494,13 @@
 
     level1.residual(g1.oz, g1.oz + n1, vb, b1, None, keep1)
     for comp in range(3):
-        packed(va, comp, comp)
-
-    here = pl.ds(pl.multiple_of((s * nc + c) * 16, 16), 16)
-    gather[here, :] = pack[...]
-
-    def spread(a, b):
-        target = (beside(s, a, ns), beside(c, b, nc))
-        pltpu.make_async_remote_copy(
-            src_ref=gather.at[here], dst_ref=gather.at[here], send_sem=gsend, recv_sem=grecv,
-            device_id=target, device_id_type=pl.DeviceIdType.MESH).start()
-
-    others(ns, nc, spread)
-    all_others = pl.ds(0, (ns * nc - 1) * 16)
-    everything = pltpu.make_async_remote_copy(
-        src_ref=gather.at[all_others], dst_ref=gather.at[all_others], send_sem=gsend, recv_sem=grecv,
-        device_id=(beside(s, 1, ns), c), device_id_type=pl.DeviceIdType.MESH)
-    everything.wait_recv()
+        gb[here * 3 + comp] = packed(va, comp)
+    all_b = gather(gb, 3, *take(2))
     ex_v.start([vb])
-    ex_u.start([ub, m0])
-
-    def assemble(t, carry):
-        z, pair = t // (nc // 2), t % (nc // 2)
-        first = gather[rows_of(t * 32, 16), :]
-        second = gather[rows_of(t * 32 + 16, 16), :]
-        for f in range(4):
-            value = jnp.concatenate([first[4 * f:4 * f + 4], second[4 * f:4 * f + 4]], axis=0)
-            ref, comp = (k2, 0) if f == 3 else (b2, f)
-            ref[rows_of((comp * (ns + 2) + z + 1) * y2 + pair * 8, 8), :] = value
-        return carry
-
-    if ns * nc <= 32:
-        for t in range(ns * nc // 2):
-            assemble(t, 0)
-    else:
-        lax.fori_loop(0, ns * nc // 2, assemble, 0)
-    level2.setup(1, ns + 1, None, b2, wa)
+
+    all_b.wait_recv()
+    assemble(gb, 3, b2)
+    level2.first(1, ns + 1, b2, wa)
     level2.sweep(1, ns + 1, wa, b2, wb)
 
     def keep2(comp, z, value, field):
@@ -467,15 +508,8 @@
 
     level2.residual(1, ns + 1, wb, b2, None, keep2)
 
-    def shrink3(z, carry):
-        for src, dst, comp in ((k2, k3, 0), (wa, b3, 0), (wa, b3, 1), (wa, b3, 2)):
-            start = (comp * (ns + 2) + z) * y2
-            total = src[pl.ds(start, y3, stride=2), :] + src[pl.ds(start + 1, y3, stride=2), :]
-            dst[plane3(comp, z), :] = pair_sum(pair_sum(total, 1), 4) * F32(0.125)
-        return carry
-
-    lax.fori_loop(1, ns + 1, shrink3, 0)
-    level3.setup(1, ns + 1, None, b3, xa)
+    shrink3([(wa, b3, comp) for comp in range(3)])
+    level3.first(1, ns + 1, b3, xa)
     old, new = xa, xb
     for turn in range(COARSE_SWEEPS - 1):
         level3.sweep(1, ns + 1, old, b3, new)
@@ -547,7 +581,8 @@
 
     level0.residual(g0.oz, g0.oz + n0, ua, b0, m0, emit)
 
-    everything.wait_send()
+    all_k.wait_send()
+    all_b.wait_send()
     for ex_one in rounds:
         ex_one.drain()
 
@@ -557,11 +592,12 @@
     g0 = Grid(nz, ny, 4, 4)
     g1 = Grid(nz // 2, ny // 2, 4, 4)
     ex = (
-        (g0, ((1, 3), (1, 2), (3, 2))),
-        (g1, ((1, 4),)),
-        (g1, ((3, 3),)),
-        (g0, ((3, 3), (1, 3))),
-        (g1, ((3, 4),)),
+        (g0, ((1, 1, 3),), False),
+        (g0, ((1, 1, 2), (3, 1, 2)), False),
+        (g1, ((1, 1, 4),), True),
+        (g1, ((3, 1, 3),), True),
+        (g0, ((3, 2, 3), (1, 3, 3)), False),
+        (g1, ((3, 2, 4),), True),
     )
     buf = lambda rows: pltpu.VMEM((rows, LANES), F32)
     y2, y3 = 4 * nc, 2 * nc
@@ -570,12 +606,11 @@
     scratch += [buf(g1.rows)] + [buf(3 * g1.rows)] * 3 + [buf(g1.rows)] * 8
     scratch += [buf(s2)] + [buf(3 * s2)] * 3 + [buf(3 * (ns + 2) * (y2 + 16))] + [buf(s2)] * 8
     scratch += [buf(s3)] + [buf(3 * s3)] * 3 + [buf(s3)] * 8
-    scratch += [buf(16), buf(ns * nc * 16), buf(3 * max(y2, 32))]
-    for grid, fields in ex:
-        sizes = [message(grid, dz, dy, fields)[1] for dz, dy in DIRS]
+    scratch += [pltpu.VMEM((ns * nc, 4, LANES), F32), pltpu.VMEM((ns * nc * 3, 4, LANES), F32), buf(3 * max(y2, 32))]
+    for grid, fields, pairs in ex:
+        sizes = [message(grid, dz, dy, fields, pairs)[1] for dz, dy in DIRS]
         scratch += [buf(n) for n in sizes] * 2
         scratch += [pltpu.SemaphoreType.DMA((8,))] * 2
-    scratch += [pltpu.SemaphoreType.DMA] * 2
 
     def run(*args):
         kernel(ns, nc, g0, g1, ex, *args)
@@ -583,7 +618,8 @@
     rows = 3 * nz * ny
     scratch += [buf(rows), pltpu.VMEM((nz * ny, LANES), jnp.int32), pltpu.SMEM((CLASSES,), F32),
                 pltpu.VMEM((nz * ny, LANES), jnp.int32), pltpu.SemaphoreType.DMA((4,))]
-    used = sum(4 * LANES * ref.shape[0] for ref in scratch if hasattr(ref, "shape"))
+    scratch += [pltpu.SemaphoreType.DMA] * 4
+    used = sum(4 * math.prod(ref.shape) for ref in scratch if hasattr(ref, "shape"))
     vmem = pl.BlockSpec(memory_space=pltpu.VMEM)
     u, r = pl.pallas_call(
         run,
@@ -593,7 +629,8 @@
         scratch_shapes=scratch,
         compiler_params=pltpu.CompilerParams(collective_id=0, has_side_effects=True, vmem_limit_bytes=used + 8 * 1024 * 1024),
         name="vcycle",
-    )(load.reshape(rows, nx), density.reshape(nz * ny, nx), moduli, fixed.reshape(nz * ny, nx))
+    )(*[pltpu.with_memory_space_constraint(a, pltpu.HBM) for a in (
+        load.reshape(rows, nx), density.reshape(nz * ny, nx), moduli, fixed.reshape(nz * ny, nx))])
     shape = (3, nz, ny, nx)
     return u.reshape(shape), r.reshape(shape)
 

time: 47.5 us -> 39.4 us (0.83)
  the two profiles are of different devices: /device:TPU:9 before, /device:TPU:0 now
where the time goes in v5:
time: 39.4 us; the launch traced here: 39.2 us
  Pallas kernels  37.1 us (94%)
  local copies, waits for them, and re-layouts  1.49 us (4%)
  between operations  0.64 us (2%)
    pallas_call x1, Pallas kernels, on_device(): pl.pallas_call(run, out_shape=[jax.ShapeDtypeStruct((rows, nx), F32)] * 2...  37.1 us
    unnamed x2, local copies, waits for them, and re-layouts  1.49 us

profile of v5, /device:TPU:0, one launch (start us, length us, event | category | flops | bytes accessed | tf_op | source)
XLA Modules:
  0.0 39.2 jit_solution(7417290618392505416)
XLA Ops:
  0.6 37.1 %vcycle.1 = (f32[768,128]{1,0:T(8,128)S(1)}, f32[768,128]{1,0:T(8,128)S(1)}) custom-call(f32[768,128]{1,0:T(8,128)} %bitcast.7, s32[256,128]{1,0:T(8,128)} %bitcast.8, f32[8]{0:T(128)} %args_2_.4, s32[256,128]{1,0:T(8,128)} %bitcast.9), custom_call_target="tpu_custom_call" | custom-call | tf_op jit(solution)/shard_map/vcycle/pallas_call | solution.py:624
  37.7 0.7 %copy.8 = f32[3,16,16,128]{3,2,1,0:T(8,128)} copy(f32[3,16,16,128]{3,2,1,0:T(8,128)S(1)} %bitcast.6) | data formatting | bytes 786432
  38.5 0.7 %copy.9 = f32[3,16,16,128]{3,2,1,0:T(8,128)} copy(f32[3,16,16,128]{3,2,1,0:T(8,128)S(1)} %bitcast.5) | data formatting | bytes 786432

commit v6 on v5

--- a/solution.py
+++ b/solution.py
@@ -126,33 +126,34 @@
     def start(self, refs):
         for d, (dz, dy) in enumerate(DIRS):
             parts, _ = message(self.grid, dz, dy, self.fields, self.pairs)
-
+            for runs, at in parts:
+                values = [refs[field][window(self.grid, comp, z, y, count, along), :]
+                          for field, comp, (z, y, _, _, count, along) in runs]
+                value = values[0]
+                if len(values) == 2:
+                    value = jnp.where(lane_iota(value.shape[0]) % 2 == 0, value, values[1])
+                self.send[d][pl.ds(at, value.shape[0]), :] = value
+        for d, (dz, dy) in enumerate(DIRS):
             @pl.when(self.exists(dz, dy))
             def _():
-                for runs, at in parts:
-                    values = [refs[field][window(self.grid, comp, z, y, count, along), :]
-                              for field, comp, (z, y, _, _, count, along) in runs]
-                    value = values[0]
-                    if len(values) == 2:
-                        value = jnp.where(lane_iota(value.shape[0]) % 2 == 0, value, values[1])
-                    self.send[d][pl.ds(at, value.shape[0]), :] = value
                 self.copy(d).start()
 
     def finish(self, refs):
         for d, (dz, dy) in enumerate(DIRS):
-            parts, _ = message(self.grid, dz, dy, self.fields, self.pairs)
-
             @pl.when(self.exists(-dz, -dy))
             def _():
                 self.copy(d).wait_recv()
-                for runs, at in parts:
-                    value = self.recv[d][pl.ds(at, runs[0][2][4]), :]
-                    values = [value]
-                    if len(runs) == 2:
-                        even = lane_iota(value.shape[0]) % 2 == 0
-                        values = [jnp.where(even, value, right(value, 1)), jnp.where(even, left(value, 1), value)]
-                    for (field, comp, (_, _, z, y, count, along)), value in zip(runs, values):
-                        refs[field][window(self.grid, comp, z, y, count, along), :] = value
+        for d, (dz, dy) in enumerate(DIRS):
+            parts, _ = message(self.grid, dz, dy, self.fields, self.pairs)
+            here = self.exists(-dz, -dy)
+            for runs, at in parts:
+                value = jnp.where(here, self.recv[d][pl.ds(at, runs[0][2][4]), :], 0.0)
+                values = [value]
+                if len(runs) == 2:
+                    even = lane_iota(value.shape[0]) % 2 == 0
+                    values = [jnp.where(even, value, right(value, 1)), jnp.where(even, left(value, 1), value)]
+                for (field, comp, (_, _, z, y, count, along)), value in zip(runs, values):
+                    refs[field][window(self.grid, comp, z, y, count, along), :] = value
 
     def drain(self):
         for d, (dz, dy) in enumerate(DIRS):
@@ -356,23 +357,30 @@
     for ref in (k0, m0, b0, k1):
         zero(ref)
 
-    def fill(get, z):
+    wide = lambda v: jnp.concatenate(
+        [jnp.zeros((g0.oy, LANES), F32), v, jnp.zeros((g0.oy, LANES), F32)], axis=0)
+    own_plane = lambda comp, z: rows_of((comp * n0 + z) * y0, y0)
+
+    def fill_stiffness(get, z):
         d = get(dens, 0, 0)
         value = jnp.zeros((y0, LANES), F32)
         for klass in range(CLASSES):
             value = jnp.where(d == klass, moduli[klass], value)
+        return [(k0, g0.plane(0, z + g0.oz), wide(value))]
+
+    def fill_rest(get, z):
         keep = 1.0 - get(fixed, 0, 0).astype(F32)
-        wide = lambda v: jnp.concatenate(
-            [jnp.zeros((g0.oy, LANES), F32), v, jnp.zeros((g0.oy, LANES), F32)], axis=0)
-        p = g0.plane(0, z + g0.oz)
-        return [(k0, p, wide(value)), (m0, p, wide(keep))] + [
+        return [(m0, g0.plane(0, z + g0.oz), wide(keep))] + [
             (b0, g0.plane(comp, z + g0.oz), wide(get(load, comp, 0))) for comp in range(3)]
 
-    for fetch in fetches:
+    for fetch in fetches[:2]:
         fetch.wait()
-    loop(0, n0, y0, lambda comp, z: rows_of((comp * n0 + z) * y0, y0), fill)
+    loop(0, n0, y0, own_plane, fill_stiffness)
     pl.semaphore_wait(barrier, ns * nc - 1)
     ex_s.start([k0])
+    for fetch in fetches[2:]:
+        fetch.wait()
+    loop(0, n0, y0, own_plane, fill_rest)
     ex_a.start([m0, b0])
 
     def coarser(src, grid, comp, z, y, count, steps):
@@ -489,6 +497,8 @@
     level1.first(g1.oz - 2, g1.oz + n1 + 2, b1, va)
     level1.sweep(g1.oz - 1, g1.oz + n1 + 1, va, b1, vb)
 
+    ex_v.start([vb])
+
     def keep1(comp, z, value, field):
         return [(va, g1.plane(comp, z), value)]
 
@@ -496,7 +506,11 @@
     for comp in range(3):
         gb[here * 3 + comp] = packed(va, comp)
     all_b = gather(gb, 3, *take(2))
-    ex_v.start([vb])
+    ex_u.finish([ub, m0])
+    ex_v.finish([vb])
+    all_k.wait_send()
+    for ex_one in rounds:
+        ex_one.drain()
 
     all_b.wait_recv()
     assemble(gb, 3, b2)
@@ -537,7 +551,6 @@
     level2.sweep(1, ns + 1, wb, b2, wa)
     level2.sweep(1, ns + 1, wa, b2, wf, wide2)
 
-    ex_v.finish([vb])
     lane8 = lane_iota(8)
     odd = c % 2 == 1
 
@@ -559,8 +572,6 @@
     level1.sweep(g1.oz - 3, g1.oz + n1 + 3, va, b1, vb)
     level1.sweep(g1.oz - 2, g1.oz + n1 + 2, vb, b1, va)
 
-    ex_u.finish([ub, m0])
-
     def add0(i, carry):
         spots = [twice(va[g1.plane(comp, i + g1.oz - 2), :][2:14], comp * g0.y) for comp in range(3)]
         for comp in range(3):
@@ -581,10 +592,15 @@
 
     level0.residual(g0.oz, g0.oz + n0, ua, b0, m0, emit)
 
-    all_k.wait_send()
     all_b.wait_send()
-    for ex_one in rounds:
-        ex_one.drain()
+
+
+def hand_over(u, r, out_u, out_r, sems):
+    copies = [pltpu.make_async_copy(src, dst, sems.at[i]) for i, (src, dst) in enumerate(((u, out_u), (r, out_r)))]
+    for one in copies:
+        one.start()
+    for one in copies:
+        one.wait()
 
 
 def on_device(ns, nc, load, density, moduli, fixed):
@@ -631,6 +647,15 @@
         name="vcycle",
     )(*[pltpu.with_memory_space_constraint(a, pltpu.HBM) for a in (
         load.reshape(rows, nx), density.reshape(nz * ny, nx), moduli, fixed.reshape(nz * ny, nx))])
+    both = pl.BlockSpec(memory_space=pltpu.HBM)
+    u, r = pl.pallas_call(
+        hand_over,
+        out_shape=[jax.ShapeDtypeStruct((rows, nx), F32)] * 2,
+        in_specs=[vmem, vmem],
+        out_specs=[both, both],
+        scratch_shapes=[pltpu.SemaphoreType.DMA((2,))],
+        name="hand_over",
+    )(*[pltpu.with_memory_space_constraint(a, pltpu.VMEM) for a in (u, r)])
     shape = (3, nz, ny, nx)
     return u.reshape(shape), r.reshape(shape)
 

time: 39.4 us -> 38.7 us (0.982)
  local copies, waits for them, and re-layouts: 1.49 us -> 0 us
  Pallas kernels: 37.1 us -> 37.9 us
    unnamed x2 -> x0, local copies, waits for them, and re-layouts: 1.49 us -> none
    pallas_call x0 -> x1, Pallas kernels: none -> 0.89 us  [on_device(): pl.pallas_call(hand_over, out_shape=[jax.ShapeDtypeStruct((rows, nx), F32...]
where the time goes in v6:
time: 38.7 us; the launch traced here: 38.6 us
  Pallas kernels  37.9 us (98%)
  between operations  0.64 us (2%)
    pallas_call x1, Pallas kernels, on_device(): pl.pallas_call(run, out_shape=[jax.ShapeDtypeStruct((rows, nx), F32)] * 2...  37 us
    pallas_call x1, Pallas kernels, on_device(): pl.pallas_call(hand_over, out_shape=[jax.ShapeDtypeStruct((rows, nx), F32...  0.89 us

profile of v6, /device:TPU:0, one launch (start us, length us, event | category | flops | bytes accessed | tf_op | source)
XLA Modules:
  0.0 38.6 jit_solution(939739418371778885)
XLA Ops:
  0.6 37.0 %vcycle.1 = (f32[768,128]{1,0:T(8,128)S(1)}, f32[768,128]{1,0:T(8,128)S(1)}) custom-call(f32[768,128]{1,0:T(8,128)} %bitcast.5, s32[256,128]{1,0:T(8,128)} %bitcast.6, f32[8]{0:T(128)} %args_2_.4, s32[256,128]{1,0:T(8,128)} %bitcast.7), custom_call_target="tpu_custom_call" | custom-call | tf_op jit(solution)/shard_map/vcycle/pallas_call | solution.py:640
  37.7 0.9 %hand_over.1 = (f32[768,128]{1,0:T(8,128)}, f32[768,128]{1,0:T(8,128)}) custom-call(f32[768,128]{1,0:T(8,128)S(1)} %get-tuple-element.6.u, f32[768,128]{1,0:T(8,128)S(1)} %get-tuple-element.7.r), custom_call_target="tpu_custom_call" | custom-call | tf_op jit(solution)/shard_map/hand_over/pallas_call | solution.py:651

commit v7 on v6

--- a/solution.py
+++ b/solution.py
@@ -13,7 +13,7 @@
 COARSE_SWEEPS = 8
 LANES = 128
 F32 = jnp.float32
-LIVE = 27
+LIVE = 36
 DIRS = ((0, 1), (0, -1), (1, 0), (-1, 0), (1, 1), (1, -1), (-1, 1), (-1, -1))
 
 
@@ -435,11 +435,6 @@
         else:
             lax.fori_loop(0, ns * nc // 2, one, 0)
 
-    gk[here] = packed(k1, 0)
-    all_k = gather(gk, 1, *take(2))
-    for ref in (ua, ub, b1, va, vb):
-        zero(ref)
-
     level0 = Level(1.0, 1, 0, 0, g0.y, False, g0.plane, k0, c0)
     level1 = Level(0.25, 2, 0, 0, g1.y, False, g1.plane, k1, c1)
     y2, y3 = 4 * nc, 2 * nc
@@ -448,15 +443,18 @@
     wide2 = lambda comp, z: rows_of((comp * (ns + 2) + z) * (y2 + 16) + 8, y2)
     level2 = Level(0.25**2, 4, 1, 4, y2, True, plane2, k2, c2)
     level3 = Level(0.25**3, 8, 2, 4, y3, True, plane3, k3, c3)
+    ex_s.finish([k0])
+    level0.setup(g0.oz - 2, g0.oz + n0 + 2)
+    gk[here] = packed(k1, 0)
+    all_k = gather(gk, 1, *take(2))
+    for ref in (ua, ub, b1, va, vb):
+        zero(ref)
     for ref, comps, plane, rows in ((k2, 1, plane2, y2), (wa, 3, plane2, y2), (wb, 3, plane2, y2),
                                     (k3, 1, plane3, y3), (xa, 3, plane3, y3), (xb, 3, plane3, y3),
                                     (wf, 3, lambda comp, z: rows_of((comp * (ns + 2) + z) * (y2 + 16), y2 + 16), y2 + 16)):
         for comp in range(comps):
             for z in (0, ns + 1):
                 ref[plane(comp, z), :] = jnp.zeros((rows, LANES), F32)
-
-    ex_s.finish([k0])
-    level0.setup(g0.oz - 2, g0.oz + n0 + 2)
     ex_a.finish([m0, b0])
     level0.first(g0.oz - 2, g0.oz + n0 + 2, b0, ua, m0)
     level0.sweep(g0.oz - 1, g0.oz + n0 + 1, ua, b0, ub)
@@ -492,8 +490,8 @@
 
     shrink3([(k2, k3, 0)])
     level3.setup(1, ns + 1)
+    ex_u.start([ub, m0])
     ex_b.finish([b1])
-    ex_u.start([ub, m0])
     level1.first(g1.oz - 2, g1.oz + n1 + 2, b1, va)
     level1.sweep(g1.oz - 1, g1.oz + n1 + 1, va, b1, vb)
 

time: 38.7 us -> 35.8 us (0.925)
  Pallas kernels: 37.9 us -> 34.9 us
    pallas_call x1, Pallas kernels: 37 us -> 34.1 us  [on_device(): pl.pallas_call(run, out_shape=[jax.ShapeDtypeStruct((rows, nx), F32)] * 2...]
where the time goes in v7:
time: 35.8 us; the launch traced here: 35.6 us
  Pallas kernels  34.9 us (97%)
  between operations  0.64 us (2%)
    pallas_call x1, Pallas kernels, on_device(): pl.pallas_call(run, out_shape=[jax.ShapeDtypeStruct((rows, nx), F32)] * 2...  34.1 us
    pallas_call x1, Pallas kernels, on_device(): pl.pallas_call(hand_over, out_shape=[jax.ShapeDtypeStruct((rows, nx), F32...  0.89 us

profile of v7, /device:TPU:0, one launch (start us, length us, event | category | flops | bytes accessed | tf_op | source)
XLA Modules:
  0.0 35.6 jit_solution(16716793302123798592)
XLA Ops:
  0.6 34.1 %vcycle.1 = (f32[768,128]{1,0:T(8,128)S(1)}, f32[768,128]{1,0:T(8,128)S(1)}) custom-call(f32[768,128]{1,0:T(8,128)} %bitcast.5, s32[256,128]{1,0:T(8,128)} %bitcast.6, f32[8]{0:T(128)} %args_2_.4, s32[256,128]{1,0:T(8,128)} %bitcast.7), custom_call_target="tpu_custom_call" | custom-call | tf_op jit(solution)/shard_map/vcycle/pallas_call | solution.py:638
  34.7 0.9 %hand_over.1 = (f32[768,128]{1,0:T(8,128)}, f32[768,128]{1,0:T(8,128)}) custom-call(f32[768,128]{1,0:T(8,128)S(1)} %get-tuple-element.6.u, f32[768,128]{1,0:T(8,128)S(1)} %get-tuple-element.7.r), custom_call_target="tpu_custom_call" | custom-call | tf_op jit(solution)/shard_map/hand_over/pallas_call | solution.py:649

commit v8 on v7

--- a/solution.py
+++ b/solution.py
@@ -13,7 +13,7 @@
 COARSE_SWEEPS = 8
 LANES = 128
 F32 = jnp.float32
-LIVE = 36
+LIVE = 48
 DIRS = ((0, 1), (0, -1), (1, 0), (-1, 0), (1, 1), (1, -1), (-1, 1), (-1, -1))
 
 

time: 35.8 us -> 35.7 us (level)
  no operation moved by 1% of the time
where the time goes in v8:
time: 35.7 us; the launch traced here: 35.6 us
  Pallas kernels  35 us (98%)
  between operations  0.64 us (2%)
    pallas_call x1, Pallas kernels, on_device(): pl.pallas_call(run, out_shape=[jax.ShapeDtypeStruct((rows, nx), F32)] * 2...  34.1 us
    pallas_call x1, Pallas kernels, on_device(): pl.pallas_call(hand_over, out_shape=[jax.ShapeDtypeStruct((rows, nx), F32...  0.89 us

profile of v8, /device:TPU:0, one launch (start us, length us, event | category | flops | bytes accessed | tf_op | source)
XLA Modules:
  0.0 35.6 jit_solution(1657321283777201153)
XLA Ops:
  0.6 34.1 %vcycle.1 = (f32[768,128]{1,0:T(8,128)S(1)}, f32[768,128]{1,0:T(8,128)S(1)}) custom-call(f32[768,128]{1,0:T(8,128)} %bitcast.5, s32[256,128]{1,0:T(8,128)} %bitcast.6, f32[8]{0:T(128)} %args_2_.4, s32[256,128]{1,0:T(8,128)} %bitcast.7), custom_call_target="tpu_custom_call" | custom-call | tf_op jit(solution)/shard_map/vcycle/pallas_call | solution.py:638
  34.7 0.9 %hand_over.1 = (f32[768,128]{1,0:T(8,128)}, f32[768,128]{1,0:T(8,128)}) custom-call(f32[768,128]{1,0:T(8,128)S(1)} %get-tuple-element.6.u, f32[768,128]{1,0:T(8,128)S(1)} %get-tuple-element.7.r), custom_call_target="tpu_custom_call" | custom-call | tf_op jit(solution)/shard_map/hand_over/pallas_call | solution.py:649

commit v9 on v7

--- a/solution.py
+++ b/solution.py
@@ -393,9 +393,6 @@
             total = pair_sum(total, step)
         return total * F32(0.125)
 
-    for z in range(n1):
-        k1[pl.ds(g1.row(0, z, 0), y1), :] = coarser(k0, g0, 0, z, 0, y1, (1,))
-    ex_k.start([k1])
 
     lane4 = lane_iota(4) % 4
 
@@ -445,6 +442,9 @@
     level3 = Level(0.25**3, 8, 2, 4, y3, True, plane3, k3, c3)
     ex_s.finish([k0])
     level0.setup(g0.oz - 2, g0.oz + n0 + 2)
+    for z in range(n1):
+        k1[pl.ds(g1.row(0, z, 0), y1), :] = coarser(k0, g0, 0, z, 0, y1, (1,))
+    ex_k.start([k1])
     gk[here] = packed(k1, 0)
     all_k = gather(gk, 1, *take(2))
     for ref in (ua, ub, b1, va, vb):

time: 35.8 us -> 35.8 us (level)
  no operation moved by 1% of the time
where the time goes in v9:
time: 35.8 us; the launch traced here: 35.6 us
  Pallas kernels  34.9 us (97%)
  between operations  0.64 us (2%)
    pallas_call x1, Pallas kernels, on_device(): pl.pallas_call(run, out_shape=[jax.ShapeDtypeStruct((rows, nx), F32)] * 2...  34 us
    pallas_call x1, Pallas kernels, on_device(): pl.pallas_call(hand_over, out_shape=[jax.ShapeDtypeStruct((rows, nx), F32...  0.89 us

profile of v9, /device:TPU:0, one launch (start us, length us, event | category | flops | bytes accessed | tf_op | source)
XLA Modules:
  0.0 35.6 jit_solution(2476457105324989916)
XLA Ops:
  0.6 34.0 %vcycle.1 = (f32[768,128]{1,0:T(8,128)S(1)}, f32[768,128]{1,0:T(8,128)S(1)}) custom-call(f32[768,128]{1,0:T(8,128)} %bitcast.5, s32[256,128]{1,0:T(8,128)} %bitcast.6, f32[8]{0:T(128)} %args_2_.4, s32[256,128]{1,0:T(8,128)} %bitcast.7), custom_call_target="tpu_custom_call" | custom-call | tf_op jit(solution)/shard_map/vcycle/pallas_call | solution.py:638
  34.7 0.9 %hand_over.1 = (f32[768,128]{1,0:T(8,128)}, f32[768,128]{1,0:T(8,128)}) custom-call(f32[768,128]{1,0:T(8,128)S(1)} %get-tuple-element.6.u, f32[768,128]{1,0:T(8,128)S(1)} %get-tuple-element.7.r), custom_call_target="tpu_custom_call" | custom-call | tf_op jit(solution)/shard_map/hand_over/pallas_call | solution.py:649
